TPU v7x, 128 devices: a whole 4x4x4 slice. The times are simulated.
128 devices in a mesh: gx: 4 (over z), gy: 32 (over x, y, core).
Axes of the slice: x: 4, y: 4, z: 4, core: 2. Of those that a mesh axis runs over, the one named last changes fastest.
Arguments:
- leaf_multipole: bfloat16 [152, 32768], P(None, ('gx', 'gy')), may hold values from -6 to 6
- up_matrices: bfloat16 [8, 152, 152], replicated, may hold values from -0.15625 to 0.15625
- down_matrices: bfloat16 [8, 152, 152], replicated, may hold values from -0.5 to 0.5
- far_matrices: bfloat16 [316, 152, 152], replicated, may hold values from -0.02734375 to 0.02734375
- send_leaf: int32 [32768], P(('gx', 'gy')), may hold values from 0 to 255
- send_parent: int32 [4096], P(('gx', 'gy')), may hold values from 0 to 31
- codes_leaf: int32 [316, 32768], P(None, ('gx', 'gy')), may hold values from 0 to 2047
- valid_leaf: int32 [316, 32768], P(None, ('gx', 'gy')), may hold values 0 or 1
- codes_parent: int32 [316, 4096], P(None, ('gx', 'gy')), may hold values from 0 to 255
- valid_parent: int32 [316, 4096], P(None, ('gx', 'gy')), may hold values 0 or 1
- codes_coarse: int32 [316, 512], P(None, ('gx', 'gy')), may hold values from 0 to 511
- valid_coarse: int32 [316, 512], P(None, ('gx', 'gy')), may hold values 0 or 1
Outputs:
- far_local: float32 [152, 32768], P(None, ('gx', 'gy'))
Inputs may be any that keep to these rules, and one draw needn't show every extreme that they name: `send_leaf`: local box indices of the sending device. `send_parent`: local box indices of the sending device. `codes_leaf`: columns of the target's own device's source table. `codes_parent`: columns of the target's own device's source table.
All inputs are finite; a program needn't handle non-finite values. No bound on the sum of `valid_leaf` or of `valid_parent` or of `valid_coarse` on one device may be relied on, other than what follows from the above.
Results may differ from a plain program's by a relative error of at most 0.0033.
Values may be sent and summed in bfloat16 or wider, within the bound.
No kernel may reach another device: no remote copies, remote signals or barrier semaphores. Data moves between devices by JAX's collectives and lax.ppermute only.
A program may use at most 192 MiB of HBM per device.

v0:
```python
import jax
import jax.numpy as jnp
from jax import lax
from jax.sharding import PartitionSpec as P


def swapped(array, axis, distance):
    return lax.ppermute(array, axis, [(i, i ^ 1 << distance) for i in range(lax.axis_size(axis))])


def upward(matrices, children):
    groups = children.shape[1] // 8
    shaped = children.reshape(children.shape[0], 8, groups)
    return jnp.einsum("cpq,qcj->pj", matrices, shaped, preferred_element_type=jnp.float32).astype(
        jnp.bfloat16
    )


def interact(stacked, table, codes, valid):
    source_rows = jnp.transpose(table)
    picked = jnp.take(source_rows, jnp.transpose(codes), axis=0)
    picked = jnp.where(jnp.transpose(valid)[:, :, None] > 0, picked, jnp.zeros((), jnp.bfloat16))
    flat = picked.reshape(picked.shape[0], stacked.shape[0])
    product = jnp.dot(flat, stacked, preferred_element_type=jnp.float32)
    return jnp.transpose(product)


def inherit(down_matrices, coarser):
    count = coarser.shape[1]
    spread = jnp.einsum("cpq,qk->pck", down_matrices, coarser, preferred_element_type=jnp.float32)
    return spread.reshape(down_matrices.shape[1], 8 * count)


def ghost_table(multipoles, send_list):
    outgoing = jnp.take(multipoles, send_list, axis=1)
    blocks = [multipoles]
    low_bits = lax.axis_size("gy").bit_length() - 1
    high_bits = lax.axis_size("gx").bit_length() - 1
    for bit_index in range(low_bits):
        blocks.append(swapped(outgoing, "gy", bit_index))
    for bit_index in range(high_bits):
        blocks.append(swapped(outgoing, "gx", bit_index))
    return jnp.concatenate(blocks, axis=1)


def shards(
    leaf_multipole,
    up_matrices,
    down_matrices,
    far_matrices,
    send_leaf,
    send_parent,
    codes_leaf,
    valid_leaf,
    codes_parent,
    valid_parent,
    codes_coarse,
    valid_coarse,
):
    offsets, width = (far_matrices.shape[0], far_matrices.shape[1])
    stacked = jnp.transpose(far_matrices, (0, 2, 1)).reshape(offsets * width, width)
    parent_mult = upward(up_matrices, leaf_multipole)
    coarse_mult = upward(up_matrices, parent_mult)
    coarse_all = lax.all_gather(coarse_mult, ("gx", "gy"), axis=1, tiled=True)
    coarse_local = interact(stacked, coarse_all, codes_coarse, valid_coarse).astype(jnp.bfloat16)
    parent_table = ghost_table(parent_mult, send_parent)
    parent_local = 2.0 * interact(stacked, parent_table, codes_parent, valid_parent) + inherit(
        down_matrices, coarse_local
    )
    parent_local = parent_local.astype(jnp.bfloat16)
    leaf_table = ghost_table(leaf_multipole, send_leaf)
    return 4.0 * interact(stacked, leaf_table, codes_leaf, valid_leaf) + inherit(
        down_matrices, parent_local
    )


def solution(mesh):
    return jax.shard_map(
        shards,
        mesh=mesh,
        in_specs=(
            P(None, ("gx", "gy")),
            P(),
            P(),
            P(),
            P(("gx", "gy")),
            P(("gx", "gy")),
            P(None, ("gx", "gy")),
            P(None, ("gx", "gy")),
            P(None, ("gx", "gy")),
            P(None, ("gx", "gy")),
            P(None, ("gx", "gy")),
            P(None, ("gx", "gy")),
        ),
        out_specs=P(None, ("gx", "gy")),
        check_vma=False,
    )
```

profile of v0, /device:TPU:1, one launch (start us, length us, event | category | flops | bytes accessed | tf_op | source)
XLA Modules:
  0.0 604.2 jit_solution(17319711847186987300)
XLA Ops:
  1.4 1.0 copy.34
  4.1 1.4 collective-permute-start.7
  5.6 1.4 collective-permute-start.8
  7.0 2.6 collective-permute-start.9
  9.6 1.2 collective-permute-start.10
  10.8 2.5 collective-permute-start.11
  15.5 1.4 compare_and_fusion.1
  16.9 1.2 compare_and_fusion.4
  18.1 1.0 compare_select_fusion
  19.1 1.1 compare_and_fusion
  20.6 35.5 %all-gather = bf16[128,4,152]{2,1,0:T(4,128)(2,1)S(1)} all-gather(bf16[1,4,152]{2,1,0:T(4,128)(2,1)S(1)} %fusion.76), channel_id=1, replica_groups=mesh['gx'=4,'gy'=32] {'gx','gy'}, dimensions={0}, use_global_device_ids=true | all-gather | bytes 156864 | tf_op jit(solution)/shard_map/all_gather | solution.py:64
  56.4 4.3 gather_fusion.4
  62.8 1.2 gather_fusion
  64.5 1.0 compare_bitcast_fusion
  65.6 8.7 %fusion.77 = bf16[4,152,1]{1,0,2:T(4,128)(2,1)S(1)} fusion(bf16[316,152,152]{0,1,2:T(8,128)(2,1)} %bitcast.107, bf16[4,316,152]{1,0,2:T(4,128)(2,1)S(1)} %reshape.84, pred[4,316]{1,0:T(4,128)(4,1)S(1)} %compare_and_fusion.2, pred[4,316]{1,0:T(4,128)(4,1)S(1)} %compare_bitcast_fusion.2), kind=kOutput, calls=%fused_computation.41 | convolution fusion | flops 58791776 | bytes 14989728 | tf_op jit(solution)/shard_map/dot_general | solution.py:24
  75.5 0.8 copy.32
  76.4 1.3 collective-permute-start.12
  78.3 2.4 collective-permute-start.13
  81.5 1.4 collective-permute-start.2
  82.9 1.3 collective-permute-start.3
  84.2 2.4 collective-permute-start.4
  86.6 29.1 %gather_fusion.3 = bf16[10112,152]{1,0:T(8,128)(2,1)} fusion(bf16[256,152]{1,0:T(8,128)(2,1)S(1)} %bitcast.104, s32[10240]{0:T(1024)S(1)} %pad_clamp_fusion), kind=kCustom, calls=%fused_computation.3 | custom fusion | bytes 6188544 | tf_op jit(solution)/shard_map/jit(_take)/gather | solution.py:21
  115.7 6.3 %copy.40 = bf16[10112,152]{0,1:T(8,128)(2,1)} copy(bf16[10112,152]{1,0:T(8,128)(2,1)} %gather_fusion.3) | data formatting | bytes 6148096 | tf_op jit(solution)/shard_map/jit(_take)/gather | solution.py:21
  122.0 10.6 %reshape.76 = bf16[32,316,152]{1,0,2:T(8,128)(2,1)} reshape(bf16[10112,152]{0,1:T(8,128)(2,1)} %copy.40) | data formatting | bytes 6148096 | tf_op jit(solution)/shard_map/jit(_take)/gather | solution.py:21
  132.5 14.8 %fusion.64 = bf16[152,32,1]{0,1,2:T(8,128)(2,1)S(1)} fusion(f32[152,32]{0,1:T(8,128)S(1)} %reshape.49, bf16[316,152,152]{0,1,2:T(8,128)(2,1)} %bitcast.108, bf16[32,316,152]{1,0,2:T(8,128)(2,1)} %reshape.76, pred[32,316]{1,0:T(8,128)(4,1)S(1)} %copy-done.5, pred[32,316]{1,0:T(8,128)(4,1)S(1)} %compare_bitcast_fusion.1), kind=kOutput, calls=%fused_computation.35 | convolution fusion | flops 470343936 | bytes 17725184 | tf_op jit(solution)/shard_map/dot_general | solution.py:24
  147.9 1.7 collective-permute-start.6
  149.8 1.9 collective-permute-done.5
  151.7 3.5 collective-permute-done.6
  155.3 318.0 %gather_fusion.1 = bf16[80896,152]{1,0:T(8,128)(2,1)} fusion(bf16[2048,152]{1,0:T(8,128)(2,1)S(1)} %bitcast.103, s32[80896]{0:T(1024)S(1)} %broadcast_clamp_fusion), kind=kCustom, calls=%fused_computation.1 | custom fusion | bytes 49508352 | tf_op jit(solution)/shard_map/jit(_take)/gather | solution.py:21
  473.3 39.6 %copy.36 = bf16[80896,152]{0,1:T(8,128)(2,1)} copy(bf16[80896,152]{1,0:T(8,128)(2,1)} %gather_fusion.1) | data formatting | bytes 49184768 | tf_op jit(solution)/shard_map/jit(_take)/gather | solution.py:21
  512.9 72.6 %reshape.60 = bf16[256,316,152]{1,0,2:T(8,128)(2,1)} reshape(bf16[80896,152]{0,1:T(8,128)(2,1)} %copy.36) | data formatting | bytes 49184768 | tf_op jit(solution)/shard_map/jit(_take)/gather | solution.py:21
  585.6 18.6 %fusion.33 = f32[152,256]{1,0:T(8,128)} fusion(f32[152,256]{1,0:T(8,128)S(1)} %copy.44, bf16[316,152,152]{0,1,2:T(8,128)(2,1)} %bitcast.109, bf16[256,316,152]{1,0,2:T(8,128)(2,1)} %reshape.60, pred[256,316]{1,0:T(8,128)(4,1)S(1)} %copy-done.4, pred[256,316]{1,0:T(8,128)(4,1)S(1)} %copy-done.3), kind=kOutput, calls=%fused_computation.26 | convolution fusion | flops 3762712576 | bytes 39667200 | tf_op jit(solution)/shard_map/dot_general | solution.py:24
  (74 shorter events, 12.0 us)
Async XLA Ops:
  0.0 3.1 copy-start
  0.0 74.3 %copy-start.2 = (bf16[8,152,152]{2,1,0:T(8,128)(2,1)S(1)}, bf16[8,152,152]{2,1,0:T(8,128)(2,1)}, u32[]{:S(2)}) copy-start(bf16[8,152,152]{2,1,0:T(8,128)(2,1)} %param.14) | copy-start | bytes 1108996
  4.1 72.2 %collective-permute-start.7 = (bf16[152,32]{0,1:T(8,128)(2,1)S(1)}, bf16[152,32]{0,1:T(8,128)(2,1)}, u32[]{:S(2)}, u32[]{:S(2)}) collective-permute-start(bf16[152,32]{0,1:T(8,128)(2,1)S(1)} %select_bitcast_fusion.1), channel_id=1, source_target_pairs={{0,1},{1,0},{2,3},{3,2},{4,5},{5,4},{6,7},{7,6},{8,9},{9,8},{10,11... | collective-permute-start | bytes 29192 | tf_op jit(solution)/shard_map/ppermute | solution.py:8
  5.6 72.8 %collective-permute-start.8 = (bf16[152,32]{0,1:T(8,128)(2,1)S(1)}, bf16[152,32]{0,1:T(8,128)(2,1)S(1)}, u32[]{:S(2)}, u32[]{:S(2)}) collective-permute-start(bf16[152,32]{0,1:T(8,128)(2,1)S(1)} %select_bitcast_fusion.1), channel_id=1, source_target_pairs={{0,2},{1,3},{2,0},{3,1},{4,6},{5,7},{6,4},{7,5},{8,10},{9,11},{10,... | collective-permute-start | bytes 29192 | tf_op jit(solution)/shard_map/ppermute | solution.py:8
  7.0 73.8 %collective-permute-start.9 = (bf16[152,32]{0,1:T(8,128)(2,1)S(1)}, bf16[152,32]{0,1:T(8,128)(2,1)S(1)}, u32[]{:S(2)}, u32[]{:S(2)}) collective-permute-start(bf16[152,32]{0,1:T(8,128)(2,1)S(1)} %select_bitcast_fusion.1), channel_id=1, source_target_pairs={{0,4},{1,5},{2,6},{3,7},{4,0},{5,1},{6,2},{7,3},{8,12},{9,13},{10,... | collective-permute-start | bytes 29192 | tf_op jit(solution)/shard_map/ppermute | solution.py:8
  9.6 71.9 %collective-permute-start.10 = (bf16[152,32]{0,1:T(8,128)(2,1)S(1)}, bf16[152,32]{0,1:T(8,128)(2,1)S(1)}, u32[]{:S(2)}, u32[]{:S(2)}) collective-permute-start(bf16[152,32]{0,1:T(8,128)(2,1)S(1)} %select_bitcast_fusion.1), channel_id=1, source_target_pairs={{0,8},{1,9},{2,10},{3,11},{4,12},{5,13},{6,14},{7,15},{8,0},{9,1},... | collective-permute-start | bytes 29192 | tf_op jit(solution)/shard_map/ppermute | solution.py:8
  10.8 70.7 %collective-permute-start.11 = (bf16[152,32]{0,1:T(8,128)(2,1)S(1)}, bf16[152,32]{0,1:T(8,128)(2,1)S(1)}, u32[]{:S(2)}, u32[]{:S(2)}) collective-permute-start(bf16[152,32]{0,1:T(8,128)(2,1)S(1)} %select_bitcast_fusion.1), channel_id=1, source_target_pairs={{0,16},{1,17},{2,18},{3,19},{4,20},{5,21},{6,22},{7,23},{8,24},{9,... | collective-permute-start | bytes 29192 | tf_op jit(solution)/shard_map/ppermute | solution.py:8
  60.8 13.7 %copy-start.6 = (pred[256]{0:T(512)(128)(4,1)S(1)}, pred[256]{0:T(512)(128)(4,1)}, u32[]{:S(2)}) copy-start(pred[256]{0:T(512)(128)(4,1)} %compare_and_fusion.4) | copy-start | bytes 772
  76.4 6.5 %collective-permute-start.12 = (bf16[152,32]{0,1:T(8,128)(2,1)S(1)}, bf16[152,32]{0,1:T(8,128)(2,1)S(1)}, u32[]{:S(2)}, u32[]{:S(2)}) collective-permute-start(bf16[152,32]{0,1:T(8,128)(2,1)S(1)} %select_bitcast_fusion.1), channel_id=1, source_target_pairs={{0,32},{32,0},{64,96},{96,64},{1,33},{33,1},{65,97},{97,65},{2,34}... | collective-permute-start | bytes 29192 | tf_op jit(solution)/shard_map/ppermute | solution.py:8
  78.3 5.8 collective-permute-start.13
  80.8 67.0 %collective-permute-start = (bf16[152,256]{0,1:T(8,128)(2,1)S(1)}, bf16[152,256]{0,1:T(8,128)(2,1)S(1)}, u32[]{:S(2)}, u32[]{:S(2)}) collective-permute-start(bf16[152,256]{0,1:T(8,128)(2,1)S(1)} %select_bitcast_fusion), channel_id=1, source_target_pairs={{0,1},{1,0},{2,3},{3,2},{4,5},{5,4},{6,7},{7,6},{8,9},{9,8},{10,11... | collective-permute-start | bytes 233480 | tf_op jit(solution)/shard_map/ppermute | solution.py:8
  81.5 66.4 %collective-permute-start.1 = (bf16[152,256]{0,1:T(8,128)(2,1)S(1)}, bf16[152,256]{0,1:T(8,128)(2,1)S(1)}, u32[]{:S(2)}, u32[]{:S(2)}) collective-permute-start(bf16[152,256]{0,1:T(8,128)(2,1)S(1)} %select_bitcast_fusion), channel_id=1, source_target_pairs={{0,2},{1,3},{2,0},{3,1},{4,6},{5,7},{6,4},{7,5},{8,10},{9,11},{10,... | collective-permute-start | bytes 233480 | tf_op jit(solution)/shard_map/ppermute | solution.py:8
  81.5 68.2 %collective-permute-start.2 = (bf16[152,256]{0,1:T(8,128)(2,1)S(1)}, bf16[152,256]{0,1:T(8,128)(2,1)S(1)}, u32[]{:S(2)}, u32[]{:S(2)}) collective-permute-start(bf16[152,256]{0,1:T(8,128)(2,1)S(1)} %select_bitcast_fusion), channel_id=1, source_target_pairs={{0,4},{1,5},{2,6},{3,7},{4,0},{5,1},{6,2},{7,3},{8,12},{9,13},{10,... | collective-permute-start | bytes 233480 | tf_op jit(solution)/shard_map/ppermute | solution.py:8
  82.9 66.8 %collective-permute-start.3 = (bf16[152,256]{0,1:T(8,128)(2,1)S(1)}, bf16[152,256]{0,1:T(8,128)(2,1)S(1)}, u32[]{:S(2)}, u32[]{:S(2)}) collective-permute-start(bf16[152,256]{0,1:T(8,128)(2,1)S(1)} %select_bitcast_fusion), channel_id=1, source_target_pairs={{0,8},{1,9},{2,10},{3,11},{4,12},{5,13},{6,14},{7,15},{8,0},{9,1},... | collective-permute-start | bytes 233480 | tf_op jit(solution)/shard_map/ppermute | solution.py:8
  84.2 65.6 %collective-permute-start.4 = (bf16[152,256]{0,1:T(8,128)(2,1)S(1)}, bf16[152,256]{0,1:T(8,128)(2,1)S(1)}, u32[]{:S(2)}, u32[]{:S(2)}) collective-permute-start(bf16[152,256]{0,1:T(8,128)(2,1)S(1)} %select_bitcast_fusion), channel_id=1, source_target_pairs={{0,16},{1,17},{2,18},{3,19},{4,20},{5,21},{6,22},{7,23},{8,24},{9,... | collective-permute-start | bytes 233480 | tf_op jit(solution)/shard_map/ppermute | solution.py:8
  86.6 46.0 %copy-start.5 = (pred[32,316]{1,0:T(8,128)(4,1)S(1)}, pred[32,316]{1,0:T(8,128)(4,1)}, u32[]{:S(2)}) copy-start(pred[32,316]{1,0:T(8,128)(4,1)} %compare_and_fusion.1) | copy-start | bytes 30340
  147.8 3.9 collective-permute-start.5
  147.9 7.3 %collective-permute-start.6 = (bf16[152,256]{0,1:T(8,128)(2,1)S(1)}, bf16[152,256]{0,1:T(8,128)(2,1)S(1)}, u32[]{:S(2)}, u32[]{:S(2)}) collective-permute-start(bf16[152,256]{0,1:T(8,128)(2,1)S(1)} %select_bitcast_fusion), channel_id=1, source_target_pairs={{0,64},{32,96},{64,0},{96,32},{1,65},{33,97},{65,1},{97,33},{2,66}... | collective-permute-start | bytes 233480 | tf_op jit(solution)/shard_map/ppermute | solution.py:8
  512.9 72.7 %copy-start.3 = (pred[256,316]{1,0:T(8,128)(4,1)S(1)}, pred[256,316]{1,0:T(8,128)(4,1)}, u32[]{:S(2)}) copy-start(pred[256,316]{1,0:T(8,128)(4,1)} %copy.31) | copy-start | bytes 242692
  512.9 72.7 %copy-start.4 = (pred[256,316]{1,0:T(8,128)(4,1)S(1)}, pred[256,316]{1,0:T(8,128)(4,1)}, u32[]{:S(2)}) copy-start(pred[256,316]{1,0:T(8,128)(4,1)} %copy.32) | copy-start | bytes 242692
  585.6 18.7 %copy-start.1 = (bf16[8,152,152]{2,1,0:T(8,128)(2,1)S(1)}, bf16[8,152,152]{2,1,0:T(8,128)(2,1)}, u32[]{:S(2)}) copy-start(bf16[8,152,152]{2,1,0:T(8,128)(2,1)} %param.13) | copy-start | bytes 1108996
where the time goes:
time: 606 us; the launch traced here: 604 us
  local copies, waits for them, and re-layouts  487 us (80%)
  matrix products  43.3 us (7%)
  blocking collectives  35.5 us (6%)
  starting transfers between devices  20.4 us (3%)
  other arithmetic  11.8 us (2%)
    gather x9, local copies, waits for them, and re-layouts, interact(): picked = jnp.take(source_rows, jnp.transpose(codes), axis=0)  481 us
    dot_general x3, matrix products, interact(): product = jnp.dot(flat, stacked, preferred_element_type=jnp.float32)  42.2 us
    all_gather x1, blocking collectives, shards(): coarse_all = lax.all_gather(coarse_mult, ('gx', 'gy'), axis=1, tiled=True)  35.5 us
    ppermute x14, starting transfers between devices, swapped(): lax.ppermute(array, axis, [(i, i ^ 1 << distance) for i in range(lax.axis...  20.4 us
  transfers between devices with their start and end apart: 14, of which 2 were waited for; matrix products, arithmetic and copies ran while one was open for 15% of the time, Pallas kernels for 0%

commit v1 on v0

v1 whole, which is shorter than its diff:
```python
import jax
import jax.numpy as jnp
from jax import lax
from jax.experimental import pallas as pl
from jax.experimental.pallas import tpu as pltpu
from jax.sharding import PartitionSpec as P

NOFF, P_SIZE = 316, 152
SUB = 4
BLOCK = 8
NSUB = 80
NBLOCK = NSUB * SUB // BLOCK
TARGETS, ROWS = 292, 296
TABLE = 2824

def main_kernel(codes_ref, w_ref, own_ref, g0, g1, g2, g3, g4, g5, g6, pown_ref, coarse_ref, down_ref, out_ref,
                table, wbuf, c0, c1, p0, p1, acc, wsem, csem):
    nit = NBLOCK // 2
    per = NSUB // nit
    codes = (c0, c1)
    picks = (p0, p1)
    def wcopy(i):
        return pltpu.make_async_copy(w_ref.at[pl.ds(i * per, per), pl.ds(0, P_SIZE)], wbuf.at[pl.ds(i * per, per)], wsem.at[i])
    def ccopy(b, slot):
        return pltpu.make_async_copy(codes_ref.at[b], codes[slot], csem.at[slot])
    ccopy(0, 0).start()
    ccopy(1, 1).start()
    for i in range(nit):
        wcopy(i).start()
    flat = table.reshape(TABLE * 2, 128)
    def fill(base, rows):
        n = rows.shape[0]
        wide = rows.astype(jnp.float32)
        flat[pl.ds(2 * base, n, stride=2), :] = wide[:, :128]
        flat[pl.ds(2 * base + 1, n, stride=2), :] = jnp.concatenate(
            [wide[:, 128:], jnp.zeros((n, 256 - P_SIZE), jnp.float32)], axis=1)
    fill(0, own_ref[...])
    fill(2048, pown_ref[...])
    for b, g in enumerate((g0, g1, g2, g3, g4, g5, g6)):
        fill(256 + 256 * b, g[0:256, :])
        fill(2080 + 32 * b, g[256:288, :])
    fill(2304, coarse_ref[...])
    flat[2 * 2816:2 * 2824, :] = jnp.zeros((16, 128), jnp.float32)
    acc[...] = jnp.zeros_like(acc)
    for p in picks:
        for o in range(SUB):
            p[o * ROWS + TARGETS:(o + 1) * ROWS] = jnp.zeros((ROWS - TARGETS, 2, 128), jnp.float32)

    def gather(slot, first, pick):
        for o in range(SUB):
            for t in range(TARGETS):
                word = (first + o) * 384 + t
                c = codes[slot][word // 128, word % 128]
                pick[o * ROWS + t] = flat[pl.ds(c, 2), :]
    def multiply(j, pick):
        lines = pick.reshape(SUB * ROWS * 2, 128)
        parts = []
        for o in range(SUB):
            for h in range(2):
                parts.append(lines[pl.ds(o * ROWS * 2 + h, ROWS, stride=2), :].astype(jnp.bfloat16))
        x = jnp.concatenate(parts, axis=1)
        acc[...] += lax.dot_general(x, wbuf[j], (((1,), (1,)), ((), ())), preferred_element_type=jnp.float32)

    def body(i, _):
        wcopy(i).wait()
        for slot in range(2):
            ccopy(2 * i + slot, slot).wait()
            for s in range(2):
                k = slot * 2 + s
                gather(slot, s * SUB, picks[s])
                multiply(4 * i + k, picks[s])
            @pl.when(i < nit - 1)
            def _():
                ccopy(2 * i + slot + 2, slot).start()
        return 0
    lax.fori_loop(0, nit, body, 0)

    nt = (((1,), (1,)), ((), ()))
    coarse_local = acc[288:296, :].astype(jnp.bfloat16)
    spread = [lax.dot_general(coarse_local, down_ref[c], nt, preferred_element_type=jnp.float32)[0:4] for c in range(8)]
    parent_local = (2.0 * acc[256:288, :] + jnp.concatenate(spread, axis=0)).astype(jnp.bfloat16)
    for c in range(8):
        inherited = lax.dot_general(parent_local, down_ref[c], nt, preferred_element_type=jnp.float32)
        acc[c * 32:(c + 1) * 32, :] = 4.0 * acc[c * 32:(c + 1) * 32, :] + inherited
    out_ref[...] = acc[0:256, :].T

def main_call(codes, w, own, ghosts, pown, coarse, down):
    vm = pl.BlockSpec(memory_space=pltpu.VMEM)
    anyspec = pl.BlockSpec(memory_space=pl.ANY)
    return pl.pallas_call(
        main_kernel,
        in_specs=[anyspec, anyspec] + [vm] * 11,
        out_specs=vm,
        out_shape=jax.ShapeDtypeStruct((P_SIZE, 256), jnp.float32),
        scratch_shapes=[
            pltpu.VMEM((TABLE, 2, 128), jnp.float32),
            pltpu.VMEM((NSUB, P_SIZE, SUB * 256), jnp.bfloat16),
            pltpu.SMEM((24, 128), jnp.int32), pltpu.SMEM((24, 128), jnp.int32),
            pltpu.VMEM((SUB * ROWS, 2, 128), jnp.float32), pltpu.VMEM((SUB * ROWS, 2, 128), jnp.float32),
            pltpu.VMEM((ROWS, P_SIZE), jnp.float32),
            pltpu.SemaphoreType.DMA((NBLOCK // 2,)), pltpu.SemaphoreType.DMA((2,)),
        ],
        compiler_params=pltpu.CompilerParams(vmem_limit_bytes=58 << 20),
        cost_estimate=pl.CostEstimate(flops=2 * 296 * 48032 * 152, bytes_accessed=28_000_000, transcendentals=0),
    )(codes, w, own, *ghosts, pown, coarse, down)

PBLOCK, STRIDE = 16, 328


def relay_kernel(f_ref, o_ref, low, high):
    for p in range(PBLOCK):
        wide = jnp.concatenate([f_ref[p].astype(jnp.float32), jnp.zeros((256 - P_SIZE, NOFF), jnp.float32)], axis=0)
        turned = wide.T
        low[p * STRIDE:p * STRIDE + NOFF, :] = turned[:, :128]
        high[p * STRIDE:p * STRIDE + NOFF, :] = turned[:, 128:]
    for o in range(NOFF):
        at = (o % SUB) * 256
        o_ref[o // SUB, :, at:at + 128] = low[pl.ds(o, PBLOCK, stride=STRIDE), :].astype(jnp.bfloat16)
        o_ref[o // SUB, :, at + 128:at + 256] = high[pl.ds(o, PBLOCK, stride=STRIDE), :].astype(jnp.bfloat16)
    o_ref[NOFF // SUB] = jnp.zeros((PBLOCK, SUB * 256), jnp.bfloat16)


def relay(far):
    return pl.pallas_call(
        relay_kernel,
        grid=(160 // PBLOCK,),
        in_specs=[pl.BlockSpec((PBLOCK, P_SIZE, NOFF), lambda i: (i, 0, 0))],
        out_specs=pl.BlockSpec((NSUB, PBLOCK, SUB * 256), lambda i: (0, i, 0)),
        out_shape=jax.ShapeDtypeStruct((NSUB, 160, SUB * 256), jnp.bfloat16),
        scratch_shapes=[pltpu.VMEM((STRIDE * PBLOCK, 128), jnp.float32)] * 2,
        compiler_params=pltpu.CompilerParams(vmem_limit_bytes=58 << 20),
        cost_estimate=pl.CostEstimate(flops=0, bytes_accessed=45_000_000, transcendentals=0),
    )(jnp.transpose(far, (1, 2, 0)))


def swapped(array, axis, distance):
    return lax.ppermute(array, axis, [(i, i ^ 1 << distance) for i in range(lax.axis_size(axis))])


def upward(matrices, children):
    groups = children.shape[1] // 8
    shaped = children.reshape(P_SIZE, 8, groups)
    return jnp.einsum("cpq,qcj->pj", matrices, shaped, preferred_element_type=jnp.float32).astype(jnp.bfloat16)


def listed(codes, valid, base):
    return jnp.where(valid > 0, 2 * (codes + base), 2 * 2816)


def shards(
    leaf_multipole,
    up_matrices,
    down_matrices,
    far_matrices,
    send_leaf,
    send_parent,
    codes_leaf,
    valid_leaf,
    codes_parent,
    valid_parent,
    codes_coarse,
    valid_coarse,
):
    own = leaf_multipole.T
    parent_mult = upward(up_matrices, leaf_multipole)
    parent_own = parent_mult.T
    coarse_mult = upward(up_matrices, parent_mult).T
    outgoing = jnp.concatenate(
        [
            own.at[send_leaf].get(mode="promise_in_bounds"),
            parent_own.at[send_parent].get(mode="promise_in_bounds"),
        ],
        axis=0,
    )
    ghosts = [swapped(outgoing, "gy", b) for b in range(5)] + [swapped(outgoing, "gx", b) for b in range(2)]
    spread = jnp.broadcast_to(coarse_mult[None], (128, 4, P_SIZE))
    coarse_all = lax.all_to_all(spread, ("gx", "gy"), 0, 0, tiled=True).reshape(512, P_SIZE)
    codes = jnp.concatenate(
        [
            listed(codes_leaf, valid_leaf, 0),
            listed(codes_parent, valid_parent, 2048),
            listed(codes_coarse, valid_coarse, 2304),
        ],
        axis=1,
    )
    codes = jnp.pad(codes, ((0, 4), (0, 384 - TARGETS)), constant_values=2 * 2816)
    codes = codes.reshape(NBLOCK, BLOCK * 3, 128)
    return main_call(codes, relay(far_matrices), own, ghosts, parent_own, coarse_all, down_matrices)


def solution(mesh):
    spec = P(None, ("gx", "gy"))
    flat = P(("gx", "gy"))
    return jax.shard_map(
        shards,
        mesh=mesh,
        in_specs=(spec, P(), P(), P(), flat, flat, spec, spec, spec, spec, spec, spec),
        out_specs=spec,
        check_vma=False,
    )
```

time: 606 us -> 135 us (0.22)
  local copies, waits for them, and re-layouts: 487 us -> 7 us
  Pallas kernels: 0 us -> 103 us
  matrix products: 43.3 us -> 0.52 us
  blocking collectives: 35.5 us -> 0 us
  other arithmetic: 11.8 us -> 4.19 us
    gather x11 -> x2, local copies, waits for them, and re-layouts: 483 us -> 1.81 us  [the longest x1 1.15 us: shards(): own.at[send_leaf].get(mode='promise_in_bounds')]
    pallas_call x0 -> x2, Pallas kernels: none -> 103 us  [the longest x1 79.3 us: main_call(): pl.pallas_call(main_kernel, in_specs=[anyspec, anyspec] + [vm] * 11, out_...]
    dot_general x5 -> x0, matrix products: 42.7 us -> none  [the longest x3 42.2 us: interact(): product = jnp.dot(flat, stacked, preferred_element_type=jnp.float32)]
    all_gather x1 -> x0, blocking collectives: 35.5 us -> none  [shards(): coarse_all = lax.all_gather(coarse_mult, ('gx', 'gy'), axis=1, tiled=True)]
    ppermute x14 -> x7, starting transfers between devices: 20.4 us -> 13.3 us  [swapped(): lax.ppermute(array, axis, [(i, i ^ 1 << distance) for i in range(lax.axis...]
  transfers between devices with their start and end apart: 14 -> 8, of which waited for: 2 -> 0; matrix products, arithmetic and copies ran while one was open for 15% -> 4% of each run, Pallas kernels for 0% -> 18%
where the time goes in v1:
time: 135 us; the launch traced here: 134 us
  Pallas kernels  103 us (76%)
  starting transfers between devices  19.4 us (14%)
  local copies, waits for them, and re-layouts  7 us (5%)
  other arithmetic  4.19 us (3%)
    pallas_call x1, Pallas kernels, main_call(): pl.pallas_call(main_kernel, in_specs=[anyspec, anyspec] + [vm] * 11, out_...  79.3 us
    pallas_call x1, Pallas kernels, relay(): pl.pallas_call(relay_kernel, grid=(160 // PBLOCK,), in_specs=[pl.BlockSpe...  23.6 us
    ppermute x7, starting transfers between devices, swapped(): lax.ppermute(array, axis, [(i, i ^ 1 << distance) for i in range(lax.axis...  13.3 us
    all_to_all x1, starting transfers between devices, shards(): lax.all_to_all(spread, ('gx', 'gy'), 0, 0, tiled=True).reshape(512, P_SIZE)  6.03 us
  transfers between devices with their start and end apart: 8, of which 0 were waited for; matrix products, arithmetic and copies ran while one was open for 4% of the time, Pallas kernels for 18%

profile of v1, /device:TPU:1, one launch (start us, length us, event | category | flops | bytes accessed | tf_op | source)
XLA Modules:
  0.0 134.1 jit_solution(3480866551106894761)
XLA Ops:
  0.0 0.7 compare_select_fusion.1
  0.7 0.7 compare_select_fusion
  1.4 1.0 copy.19
  2.4 1.2 gather_fusion
  3.6 0.3 fusion
  3.9 0.7 gather_fusion.1
  4.6 4.5 %collective-permute-start.6 = (bf16[288,152]{1,0:T(8,128)(2,1)S(1)}, bf16[288,152]{1,0:T(8,128)(2,1)S(1)}, u32[]{:S(2)}, u32[]{:S(2)}) collective-permute-start(bf16[288,152]{1,0:T(8,128)(2,1)S(1)} %constant_dynamic-update-slice_fusion), channel_id=1, source_target_pairs={{0,64},{32,96},{64,0},{96,32},{1,65},{33,97},{65,1},{97,33},{2,66}... | collective-permute-start | bytes 262664 | tf_op jit(solution)/shard_map/ppermute | solution.py:137
  9.1 0.7 collective-permute-start.5
  9.8 2.7 %collective-permute-start.4 = (bf16[288,152]{1,0:T(8,128)(2,1)S(1)}, bf16[288,152]{1,0:T(8,128)(2,1)S(1)}, u32[]{:S(2)}, u32[]{:S(2)}) collective-permute-start(bf16[288,152]{1,0:T(8,128)(2,1)S(1)} %constant_dynamic-update-slice_fusion), channel_id=1, source_target_pairs={{0,16},{1,17},{2,18},{3,19},{4,20},{5,21},{6,22},{7,23},{8,24},{9,... | collective-permute-start | bytes 262664 | tf_op jit(solution)/shard_map/ppermute | solution.py:137
  12.5 0.3 collective-permute-start.3
  12.9 2.9 %collective-permute-start.2 = (bf16[288,152]{1,0:T(8,128)(2,1)S(1)}, bf16[288,152]{1,0:T(8,128)(2,1)S(1)}, u32[]{:S(2)}, u32[]{:S(2)}) collective-permute-start(bf16[288,152]{1,0:T(8,128)(2,1)S(1)} %constant_dynamic-update-slice_fusion), channel_id=1, source_target_pairs={{0,4},{1,5},{2,6},{3,7},{4,0},{5,1},{6,2},{7,3},{8,12},{9,13},{10,... | collective-permute-start | bytes 262664 | tf_op jit(solution)/shard_map/ppermute | solution.py:137
  15.8 0.2 fusion.1
  16.0 0.8 broadcast_in_dim.29
  16.8 6.0 %all-to-all-start = ((bf16[128,4,152]{2,1,0:T(4,128)(2,1)}), bf16[128,4,152]{2,1,0:T(4,128)(2,1)S(1)}, u32[]{:S(2)}, u32[]{:S(2)}) async-start(bf16[128,4,152]{2,1,0:T(4,128)(2,1)} %broadcast_in_dim.29), calls=%async_computation | async-start | bytes 524288 | tf_op jit(solution)/shard_map/all_to_all | solution.py:177
  22.9 0.8 multiply_select_fusion.1
  23.7 1.1 multiply_select_fusion
  24.8 0.7 multiply_select_fusion.2
  25.6 0.1 copy.17
  25.7 0.1 copy.18
  25.8 0.0 collective-permute-done.6.g6
  25.8 1.5 %collective-permute-start.1 = (bf16[288,152]{1,0:T(8,128)(2,1)S(1)}, bf16[288,152]{1,0:T(8,128)(2,1)S(1)}, u32[]{:S(2)}, u32[]{:S(2)}) collective-permute-start(bf16[288,152]{1,0:T(8,128)(2,1)S(1)} %constant_dynamic-update-slice_fusion), channel_id=1, source_target_pairs={{0,2},{1,3},{2,0},{3,1},{4,6},{5,7},{6,4},{7,5},{8,10},{9,11},{10,... | collective-permute-start | bytes 262664 | tf_op jit(solution)/shard_map/ppermute | solution.py:137
  27.3 0.6 collective-permute-start
  27.9 0.1 pad_add_fusion
  28.1 0.8 reshape.13.codes_ref
  28.9 23.6 %shard_map.118.w_ref = bf16[80,160,1024]{2,1,0:T(8,128)(2,1)} custom-call(bf16[152,152,316]{2,1,0:T(8,128)(2,1)} %bitcast.18), custom_call_target="tpu_custom_call" | custom-call | bytes 45000000 | tf_op jit(solution)/shard_map/pallas_call | solution.py:124
  52.5 0.9 reshape.16.coarse_ref
  53.5 0.6 copy-done.5
  54.0 0.1 copy-done.6
  54.1 0.1 copy-done.7
  54.1 0.0 copy-done.8
  54.2 0.7 copy-done.9
  54.8 79.3 %shard_map.119 = f32[152,256]{1,0:T(8,128)} custom-call(s32[40,24,128]{2,1,0:T(8,128)} %reshape.13.codes_ref, bf16[80,160,1024]{2,1,0:T(8,128)(2,1)} %shard_map.118.w_ref, bf16[256,152]{1,0:T(8,128)(2,1)} %bitcast.21, bf16[288,152]{1,0:T(8,128)(2,1)} %copy-done.9, bf16[288,152]{1,0:T(8,128)(2,1)} %copy-done.8, bf16[288,152]{1,0:T(8,128)(2,1)} %copy-done.7, ...), custom_call_target="tpu_custom_call" | custom-call | flops 4322111488 | bytes 28000000 | tf_op jit(solution)/shard_map/pallas_call | solution.py:90
  (27 shorter events, 0.1 us)
Async XLA Ops:
  0.0 3.6 %copy-start = (bf16[8,152,152]{2,1,0:T(8,128)(2,1)S(1)}, bf16[8,152,152]{2,1,0:T(8,128)(2,1)}, u32[]{:S(2)}) copy-start(bf16[8,152,152]{2,1,0:T(8,128)(2,1)} %param.13) | copy-start | bytes 1108996
  2.4 50.1 %copy-start.1 = (bf16[152,256]{0,1:T(8,128)(2,1)}, bf16[152,256]{0,1:T(8,128)(2,1)S(1)}, u32[]{:S(2)}) copy-start(bf16[152,256]{0,1:T(8,128)(2,1)S(1)} %copy.19) | copy-start | bytes 233476
  3.9 49.6 %copy-start.2 = (bf16[152,32]{0,1:T(8,128)(2,1)}, bf16[152,32]{0,1:T(8,128)(2,1)S(1)}, u32[]{:S(2)}) copy-start(bf16[152,32]{0,1:T(8,128)(2,1)S(1)} %fusion) | copy-start | bytes 29188
  4.6 21.3 %collective-permute-start.6 = (bf16[288,152]{1,0:T(8,128)(2,1)S(1)}, bf16[288,152]{1,0:T(8,128)(2,1)S(1)}, u32[]{:S(2)}, u32[]{:S(2)}) collective-permute-start(bf16[288,152]{1,0:T(8,128)(2,1)S(1)} %constant_dynamic-update-slice_fusion), channel_id=1, source_target_pairs={{0,64},{32,96},{64,0},{96,32},{1,65},{33,97},{65,1},{97,33},{2,66}... | collective-permute-start | bytes 262664 | tf_op jit(solution)/shard_map/ppermute | solution.py:137
  9.1 18.2 %collective-permute-start.5 = (bf16[288,152]{1,0:T(8,128)(2,1)S(1)}, bf16[288,152]{1,0:T(8,128)(2,1)S(1)}, u32[]{:S(2)}, u32[]{:S(2)}) collective-permute-start(bf16[288,152]{1,0:T(8,128)(2,1)S(1)} %constant_dynamic-update-slice_fusion), channel_id=1, source_target_pairs={{0,32},{32,0},{64,96},{96,64},{1,33},{33,1},{65,97},{97,65},{2,34}... | collective-permute-start | bytes 262664 | tf_op jit(solution)/shard_map/ppermute | solution.py:137
  9.8 43.6 %collective-permute-start.4 = (bf16[288,152]{1,0:T(8,128)(2,1)S(1)}, bf16[288,152]{1,0:T(8,128)(2,1)S(1)}, u32[]{:S(2)}, u32[]{:S(2)}) collective-permute-start(bf16[288,152]{1,0:T(8,128)(2,1)S(1)} %constant_dynamic-update-slice_fusion), channel_id=1, source_target_pairs={{0,16},{1,17},{2,18},{3,19},{4,20},{5,21},{6,22},{7,23},{8,24},{9,... | collective-permute-start | bytes 262664 | tf_op jit(solution)/shard_map/ppermute | solution.py:137
  12.5 40.8 %collective-permute-start.3 = (bf16[288,152]{1,0:T(8,128)(2,1)S(1)}, bf16[288,152]{1,0:T(8,128)(2,1)S(1)}, u32[]{:S(2)}, u32[]{:S(2)}) collective-permute-start(bf16[288,152]{1,0:T(8,128)(2,1)S(1)} %constant_dynamic-update-slice_fusion), channel_id=1, source_target_pairs={{0,8},{1,9},{2,10},{3,11},{4,12},{5,13},{6,14},{7,15},{8,0},{9,1},... | collective-permute-start | bytes 262664 | tf_op jit(solution)/shard_map/ppermute | solution.py:137
  12.9 40.5 %collective-permute-start.2 = (bf16[288,152]{1,0:T(8,128)(2,1)S(1)}, bf16[288,152]{1,0:T(8,128)(2,1)S(1)}, u32[]{:S(2)}, u32[]{:S(2)}) collective-permute-start(bf16[288,152]{1,0:T(8,128)(2,1)S(1)} %constant_dynamic-update-slice_fusion), channel_id=1, source_target_pairs={{0,4},{1,5},{2,6},{3,7},{4,0},{5,1},{6,2},{7,3},{8,12},{9,13},{10,... | collective-permute-start | bytes 262664 | tf_op jit(solution)/shard_map/ppermute | solution.py:137
  16.8 35.7 %all-to-all-start = ((bf16[128,4,152]{2,1,0:T(4,128)(2,1)}), bf16[128,4,152]{2,1,0:T(4,128)(2,1)S(1)}, u32[]{:S(2)}, u32[]{:S(2)}) async-start(bf16[128,4,152]{2,1,0:T(4,128)(2,1)} %broadcast_in_dim.29), calls=%async_computation | async-start | bytes 524288 | tf_op jit(solution)/shard_map/all_to_all | solution.py:177
  25.8 27.6 %copy-start.3 = (bf16[288,152]{1,0:T(8,128)(2,1)}, bf16[288,152]{1,0:T(8,128)(2,1)S(1)}, u32[]{:S(2)}) copy-start(bf16[288,152]{1,0:T(8,128)(2,1)S(1)} %collective-permute-done.6.g6) | copy-start | bytes 262660
  25.8 27.6 %collective-permute-start.1 = (bf16[288,152]{1,0:T(8,128)(2,1)S(1)}, bf16[288,152]{1,0:T(8,128)(2,1)S(1)}, u32[]{:S(2)}, u32[]{:S(2)}) collective-permute-start(bf16[288,152]{1,0:T(8,128)(2,1)S(1)} %constant_dynamic-update-slice_fusion), channel_id=1, source_target_pairs={{0,2},{1,3},{2,0},{3,1},{4,6},{5,7},{6,4},{7,5},{8,10},{9,11},{10,... | collective-permute-start | bytes 262664 | tf_op jit(solution)/shard_map/ppermute | solution.py:137
  27.3 26.2 %copy-start.4 = (bf16[288,152]{1,0:T(8,128)(2,1)}, bf16[288,152]{1,0:T(8,128)(2,1)S(1)}, u32[]{:S(2)}) copy-start(bf16[288,152]{1,0:T(8,128)(2,1)S(1)} %collective-permute-done.5.g5) | copy-start | bytes 262660
  27.3 26.1 %collective-permute-start = (bf16[288,152]{1,0:T(8,128)(2,1)S(1)}, bf16[288,152]{1,0:T(8,128)(2,1)S(1)}, u32[]{:S(2)}, u32[]{:S(2)}) collective-permute-start(bf16[288,152]{1,0:T(8,128)(2,1)S(1)} %constant_dynamic-update-slice_fusion), channel_id=1, source_target_pairs={{0,1},{1,0},{2,3},{3,2},{4,5},{5,4},{6,7},{7,6},{8,9},{9,8},{10,11... | collective-permute-start | bytes 262664 | tf_op jit(solution)/shard_map/ppermute | solution.py:137
  53.4 0.7 copy-start.5
  53.4 0.7 copy-start.6
  53.4 0.7 copy-start.7
  53.4 0.8 copy-start.8
  54.2 0.7 copy-start.9

commit v2 on v1

v2 whole, which is shorter than its diff:
```python
import jax
import jax.numpy as jnp
from jax import lax
from jax.experimental import pallas as pl
from jax.experimental.pallas import tpu as pltpu
from jax.sharding import PartitionSpec as P

NOFF, P_SIZE = 316, 152
BLOCK = 8
COPIED = 5
NBLOCK = 40
LEAVES, PARENTS, COARSE = 256, 32, 4
ROWS = 296
TABLE, ZERO = 2568, 2560
PADDED = 160
PIECE = 512
NT = (((1,), (1,)), ((), ()))


def main_kernel(codes_ref, lanes_ref, plane_ref, w_ref, own_ref, g0, g1, g2, g3, g4, g5, g6, pown_ref, coarse_ref,
                down_ref, out_ref, table, columns, held, ptable, wbuf, c0, c1, p0, p1, acc, turned, wsem, csem):
    nit = NBLOCK // 2
    codes, picks = (c0, c1), (p0, p1)

    def wcopy(i):
        return pltpu.make_async_copy(w_ref.at[pl.ds(i * 2, 2)], wbuf.at[pl.ds(i * 2, 2)], wsem.at[i])

    def ccopy(b, slot):
        return pltpu.make_async_copy(codes_ref.at[b], codes[slot], csem.at[slot])

    ccopy(0, 0).start()
    ccopy(1, 1).start()
    for i in range(nit):
        wcopy(i).start()
    flat = table.reshape(TABLE * 2, 128)

    def widened(rows):
        wide = rows.astype(jnp.float32)
        return jnp.concatenate([wide, jnp.zeros((rows.shape[0], 256 - P_SIZE), jnp.float32)], axis=1)

    def fill(base, wide):
        n = wide.shape[0]
        flat[pl.ds(2 * base, n, stride=2), :] = wide[:, :128]
        flat[pl.ds(2 * base + 1, n, stride=2), :] = wide[:, 128:]

    held[...] = jnp.zeros_like(held)
    for b, g in enumerate((own_ref, g0, g1, g2, g3, g4, g5, g6)):
        wide = widened(g[0:LEAVES, :])
        fill(LEAVES * b, wide)
        columns[:, LEAVES * b:LEAVES * (b + 1)] = wide.T[0:PADDED].astype(jnp.bfloat16)
    fill(2048, widened(coarse_ref[...]))
    flat[2 * ZERO:2 * TABLE, :] = jnp.zeros((2 * (TABLE - ZERO), 128), jnp.float32)
    parents = jnp.concatenate([pown_ref[...].astype(jnp.float32)] + [g[LEAVES:LEAVES + PARENTS, :].astype(jnp.float32) for g in (g0, g1, g2, g3, g4, g5, g6)], axis=0)
    ptable[...] = widened(parents).T.astype(jnp.bfloat16)
    acc[...] = jnp.zeros_like(acc)
    turned[...] = jnp.zeros_like(turned)
    for p in picks:
        for o in range(BLOCK):
            at = COPIED * LEAVES + o * 8
            p[at + COARSE:at + 8] = jnp.zeros((8 - COARSE, 2, 128), jnp.float32)

    def copy_rows(slot, start, stop):
        for word in range(start, stop):
            picks[slot][word] = flat[pl.ds(codes[slot][word // 128, word % 128], 2), :]

    def chosen(column, depth, base):
        hot = lax.broadcasted_iota(jnp.int32, (depth, column.shape[1]), 0) == column - base
        return jnp.where(hot, 1.0, 0.0).astype(jnp.bfloat16)

    def block(b, slot):
        pieces = [(o, k) for o in range(BLOCK - COPIED) for k in range(2048 // PIECE)]
        share = COPIED * LEAVES // len(pieces)
        wide = jnp.dot(ptable[...], chosen(plane_ref[b], 256, 0), preferred_element_type=jnp.float32).T
        lines = picks[slot].reshape((COPIED * LEAVES + BLOCK * 8) * 2, 128)
        for o in range(BLOCK):
            for t in range(COARSE):
                pick_row = flat[pl.ds(codes[slot][(COPIED * LEAVES) // 128, o * COARSE + t], 2), :]
                picks[slot][COPIED * LEAVES + o * 8 + t] = pick_row
        for n, (o, k) in enumerate(pieces):
            @pl.when(b >= 0)
            def _():
                hot = chosen(lanes_ref[b, COPIED + o:COPIED + o + 1, :], PIECE, k * PIECE)
                found = jnp.dot(columns[:, k * PIECE:(k + 1) * PIECE], hot, preferred_element_type=jnp.float32)
                rows = slice(o * 256, o * 256 + PADDED)
                copy_rows(slot, n * share, COPIED * LEAVES if n == len(pieces) - 1 else (n + 1) * share)
                held[rows, :] = found if k == 0 else held[rows, :] + found

        def few(o, h):
            at = COPIED * LEAVES + o * 8
            return [wide[o * PARENTS:(o + 1) * PARENTS, h * 128:h * 128 + 128], lines[pl.ds(2 * at + h, 8, stride=2), :]]

        tail = wbuf[b, :, COPIED * 256:BLOCK * 256]
        turned[...] += jnp.dot(tail, held[...].astype(jnp.bfloat16), preferred_element_type=jnp.float32)
        rest = jnp.concatenate([jnp.concatenate(few(o, h), axis=0).astype(jnp.bfloat16) for o in range(COPIED, BLOCK) for h in range(2)], axis=1)
        acc[LEAVES:ROWS, :] += lax.dot_general(rest, tail, NT, preferred_element_type=jnp.float32)
        x = jnp.concatenate(
            [
                jnp.concatenate([lines[pl.ds(o * LEAVES * 2 + h, LEAVES, stride=2), :]] + few(o, h), axis=0).astype(jnp.bfloat16)
                for o in range(COPIED)
                for h in range(2)
            ],
            axis=1,
        )
        acc[...] += lax.dot_general(x, wbuf[b, :, 0:COPIED * 256], NT, preferred_element_type=jnp.float32)

    def body(i, _):
        wcopy(i).wait()
        for slot in range(2):
            ccopy(2 * i + slot, slot).wait()
            block(2 * i + slot, slot)
            @pl.when(i < nit - 1)
            def _():
                ccopy(2 * i + slot + 2, slot).start()
        return 0

    lax.fori_loop(0, nit, body, 0)

    coarse_local = acc[288:296, 0:P_SIZE].astype(jnp.bfloat16)
    spread = [lax.dot_general(coarse_local, down_ref[c], NT, preferred_element_type=jnp.float32)[0:4] for c in range(8)]
    parent_local = (2.0 * acc[256:288, 0:P_SIZE] + jnp.concatenate(spread, axis=0)).astype(jnp.bfloat16)
    inherited = [lax.dot_general(parent_local, down_ref[c], NT, preferred_element_type=jnp.float32) for c in range(8)]
    far = 4.0 * acc[0:256, 0:P_SIZE] + jnp.concatenate(inherited, axis=0)
    out_ref[...] = far.T + 4.0 * turned[0:P_SIZE, :]


def main_call(codes, lanes, plane, w, own, ghosts, pown, coarse, down):
    vm = pl.BlockSpec(memory_space=pltpu.VMEM)
    anyspec = pl.BlockSpec(memory_space=pl.ANY)
    picked = COPIED * LEAVES + BLOCK * 8
    return pl.pallas_call(
        main_kernel,
        in_specs=[anyspec, vm, vm, anyspec] + [vm] * 11,
        out_specs=vm,
        out_shape=jax.ShapeDtypeStruct((P_SIZE, LEAVES), jnp.float32),
        scratch_shapes=[
            pltpu.VMEM((TABLE, 2, 128), jnp.float32),
            pltpu.VMEM((PADDED, 2048), jnp.bfloat16),
            pltpu.VMEM(((BLOCK - COPIED) * 256, LEAVES), jnp.float32),
            pltpu.VMEM((256, 256), jnp.bfloat16),
            pltpu.VMEM((NBLOCK, PADDED, BLOCK * 256), jnp.bfloat16),
            pltpu.SMEM((16, 128), jnp.int32), pltpu.SMEM((16, 128), jnp.int32),
            pltpu.VMEM((picked, 2, 128), jnp.float32), pltpu.VMEM((picked, 2, 128), jnp.float32),
            pltpu.VMEM((ROWS, PADDED), jnp.float32),
            pltpu.VMEM((PADDED, LEAVES), jnp.float32),
            pltpu.SemaphoreType.DMA((NBLOCK // 2,)), pltpu.SemaphoreType.DMA((2,)),
        ],
        compiler_params=pltpu.CompilerParams(vmem_limit_bytes=58 << 20),
        cost_estimate=pl.CostEstimate(flops=2 * 296 * 48032 * 152, bytes_accessed=28_000_000, transcendentals=0),
    )(codes, lanes, plane, w, own, *ghosts, pown, coarse, down)


def tables(codes_leaf, valid_leaf, codes_parent, valid_parent, codes_coarse, valid_coarse):
    grow = ((0, BLOCK * NBLOCK - NOFF), (0, 0))
    lanes = jnp.pad(jnp.where(valid_leaf > 0, codes_leaf, -1), grow, constant_values=-1).reshape(NBLOCK, BLOCK, LEAVES)
    plane = jnp.pad(jnp.where(valid_parent > 0, codes_parent, -1), grow, constant_values=-1)
    plane = plane.reshape(NBLOCK, 1, BLOCK * PARENTS)
    coarse = jnp.pad(jnp.where(valid_coarse > 0, codes_coarse + 2048, ZERO), grow, constant_values=ZERO)
    coarse = jnp.pad(coarse.reshape(NBLOCK, 1, BLOCK * COARSE), ((0, 0), (0, 15 - 2 * COPIED), (0, 128 - BLOCK * COARSE)))
    rows = lanes[:, 0:COPIED].reshape(NBLOCK, COPIED * 2, 128)
    codes = 2 * jnp.concatenate([jnp.where(rows < 0, ZERO, rows), coarse], axis=1)
    return codes, lanes, plane

PBLOCK, STRIDE = 16, 328


def relay_kernel(f_ref, o_ref, low, high):
    for p in range(PBLOCK):
        wide = jnp.concatenate([f_ref[p].astype(jnp.float32), jnp.zeros((256 - P_SIZE, NOFF), jnp.float32)], axis=0)
        turned = wide.T
        low[p * STRIDE:p * STRIDE + NOFF, :] = turned[:, :128]
        high[p * STRIDE:p * STRIDE + NOFF, :] = turned[:, 128:]
    for o in range(NOFF):
        at = (o % BLOCK) * 256
        o_ref[o // BLOCK, :, at:at + 128] = low[pl.ds(o, PBLOCK, stride=STRIDE), :].astype(jnp.bfloat16)
        o_ref[o // BLOCK, :, at + 128:at + 256] = high[pl.ds(o, PBLOCK, stride=STRIDE), :].astype(jnp.bfloat16)
    o_ref[NBLOCK - 1, :, (NOFF % BLOCK) * 256:] = jnp.zeros((PBLOCK, (BLOCK - NOFF % BLOCK) * 256), jnp.bfloat16)


def relay(far):
    return pl.pallas_call(
        relay_kernel,
        grid=(PADDED // PBLOCK,),
        in_specs=[pl.BlockSpec((PBLOCK, P_SIZE, NOFF), lambda i: (i, 0, 0))],
        out_specs=pl.BlockSpec((NBLOCK, PBLOCK, BLOCK * 256), lambda i: (0, i, 0)),
        out_shape=jax.ShapeDtypeStruct((NBLOCK, PADDED, BLOCK * 256), jnp.bfloat16),
        scratch_shapes=[pltpu.VMEM((STRIDE * PBLOCK, 128), jnp.float32)] * 2,
        compiler_params=pltpu.CompilerParams(vmem_limit_bytes=58 << 20),
        cost_estimate=pl.CostEstimate(flops=0, bytes_accessed=45_000_000, transcendentals=0),
    )(jnp.transpose(far, (1, 2, 0)))


def swapped(array, axis, distance):
    return lax.ppermute(array, axis, [(i, i ^ 1 << distance) for i in range(lax.axis_size(axis))])


def upward(matrices, children):
    groups = children.shape[1] // 8
    shaped = children.reshape(P_SIZE, 8, groups)
    return jnp.einsum("cpq,qcj->pj", matrices, shaped, preferred_element_type=jnp.float32).astype(jnp.bfloat16)


def shards(
    leaf_multipole,
    up_matrices,
    down_matrices,
    far_matrices,
    send_leaf,
    send_parent,
    codes_leaf,
    valid_leaf,
    codes_parent,
    valid_parent,
    codes_coarse,
    valid_coarse,
):
    own = leaf_multipole.T
    parent_mult = upward(up_matrices, leaf_multipole)
    parent_own = parent_mult.T
    coarse_mult = upward(up_matrices, parent_mult).T
    outgoing = jnp.concatenate(
        [
            own.at[send_leaf].get(mode="promise_in_bounds"),
            parent_own.at[send_parent].get(mode="promise_in_bounds"),
        ],
        axis=0,
    )
    ghosts = [swapped(outgoing, "gy", b) for b in range(5)] + [swapped(outgoing, "gx", b) for b in range(2)]
    spread = jnp.broadcast_to(coarse_mult[None], (128, 4, P_SIZE))
    coarse_all = lax.all_to_all(spread, ("gx", "gy"), 0, 0, tiled=True).reshape(512, P_SIZE)
    codes, lanes, plane = tables(codes_leaf, valid_leaf, codes_parent, valid_parent, codes_coarse, valid_coarse)
    return main_call(codes, lanes, plane, relay(far_matrices), own, ghosts, parent_own, coarse_all, down_matrices)


def solution(mesh):
    spec = P(None, ("gx", "gy"))
    flat = P(("gx", "gy"))
    return jax.shard_map(
        shards,
        mesh=mesh,
        in_specs=(spec, P(), P(), P(), flat, flat, spec, spec, spec, spec, spec, spec),
        out_specs=spec,
        check_vma=False,
    )
```

time: 135 us -> 129 us (0.956)
  Pallas kernels: 103 us -> 94.8 us
    pallas_call x2, Pallas kernels: 103 us -> 94.8 us  [the longest x1 71.2 us: main_call(): pl.pallas_call(main_kernel, in_specs=[anyspec, vm, vm, anyspec] + [vm] *...]
    select_n x3 -> x4, other arithmetic: 2.67 us -> 2.72 us  [the longest x1 1.12 us: tables(): jnp.where(valid_leaf > 0, codes_leaf, -1)]
  transfers between devices with their start and end apart: 8 -> 8, of which waited for: 0 -> 1; matrix products, arithmetic and copies ran while one was open for 4% -> 5% of each run, Pallas kernels for 18% -> 19%
where the time goes in v2:
time: 129 us; the launch traced here: 127 us
  Pallas kernels  94.8 us (73%)
  starting transfers between devices  19.3 us (15%)
  local copies, waits for them, and re-layouts  7.06 us (5%)
  other arithmetic  4.92 us (4%)
    pallas_call x1, Pallas kernels, main_call(): pl.pallas_call(main_kernel, in_specs=[anyspec, vm, vm, anyspec] + [vm] *...  71.2 us
    pallas_call x1, Pallas kernels, relay(): pl.pallas_call(relay_kernel, grid=(PADDED // PBLOCK,), in_specs=[pl.Block...  23.6 us
    ppermute x7, starting transfers between devices, swapped(): lax.ppermute(array, axis, [(i, i ^ 1 << distance) for i in range(lax.axis...  13.2 us
    all_to_all x1, starting transfers between devices, shards(): lax.all_to_all(spread, ('gx', 'gy'), 0, 0, tiled=True).reshape(512, P_SIZE)  6.03 us
  transfers between devices with their start and end apart: 8, of which 1 were waited for; matrix products, arithmetic and copies ran while one was open for 5% of the time, Pallas kernels for 19%

profile of v2, /device:TPU:1, one launch (start us, length us, event | category | flops | bytes accessed | tf_op | source)
XLA Modules:
  0.0 127.3 jit_solution(12598438556821091141)
XLA Ops:
  0.0 0.7 compare_select_fusion.4
  0.7 0.7 compare_select_fusion.3
  1.4 1.0 copy.20
  2.4 1.2 gather_fusion
  3.6 0.3 fusion
  3.9 0.7 gather_fusion.1
  4.6 4.5 %collective-permute-start.6 = (bf16[288,152]{1,0:T(8,128)(2,1)S(1)}, bf16[288,152]{1,0:T(8,128)(2,1)S(1)}, u32[]{:S(2)}, u32[]{:S(2)}) collective-permute-start(bf16[288,152]{1,0:T(8,128)(2,1)S(1)} %constant_dynamic-update-slice_fusion), channel_id=1, source_target_pairs={{0,64},{32,96},{64,0},{96,32},{1,65},{33,97},{65,1},{97,33},{2,66}... | collective-permute-start | bytes 262664 | tf_op jit(solution)/shard_map/ppermute | solution.py:193
  9.1 0.7 collective-permute-start.5
  9.8 2.7 %collective-permute-start.4 = (bf16[288,152]{1,0:T(8,128)(2,1)S(1)}, bf16[288,152]{1,0:T(8,128)(2,1)S(1)}, u32[]{:S(2)}, u32[]{:S(2)}) collective-permute-start(bf16[288,152]{1,0:T(8,128)(2,1)S(1)} %constant_dynamic-update-slice_fusion), channel_id=1, source_target_pairs={{0,16},{1,17},{2,18},{3,19},{4,20},{5,21},{6,22},{7,23},{8,24},{9,... | collective-permute-start | bytes 262664 | tf_op jit(solution)/shard_map/ppermute | solution.py:193
  12.5 0.3 collective-permute-start.3
  12.9 2.9 %collective-permute-start.2 = (bf16[288,152]{1,0:T(8,128)(2,1)S(1)}, bf16[288,152]{1,0:T(8,128)(2,1)S(1)}, u32[]{:S(2)}, u32[]{:S(2)}) collective-permute-start(bf16[288,152]{1,0:T(8,128)(2,1)S(1)} %constant_dynamic-update-slice_fusion), channel_id=1, source_target_pairs={{0,4},{1,5},{2,6},{3,7},{4,0},{5,1},{6,2},{7,3},{8,12},{9,13},{10,... | collective-permute-start | bytes 262664 | tf_op jit(solution)/shard_map/ppermute | solution.py:193
  15.8 0.2 fusion.1
  16.0 0.8 broadcast_in_dim.34
  16.9 6.0 %all-to-all-start = ((bf16[128,4,152]{2,1,0:T(4,128)(2,1)}), bf16[128,4,152]{2,1,0:T(4,128)(2,1)S(1)}, u32[]{:S(2)}, u32[]{:S(2)}) async-start(bf16[128,4,152]{2,1,0:T(4,128)(2,1)} %broadcast_in_dim.34), calls=%async_computation | async-start | bytes 524288 | tf_op jit(solution)/shard_map/all_to_all | solution.py:229
  22.9 1.1 compare_select_fusion.1
  24.2 0.9 compare_select_fusion.2
  25.0 0.7 add_select_fusion
  25.7 0.1 copy.24
  25.9 0.7 reshape.49.plane_ref
  26.6 0.1 copy.23
  26.8 0.1 reshape.24
  26.9 23.6 %shard_map.118.w_ref = bf16[40,160,2048]{2,1,0:T(8,128)(2,1)} custom-call(bf16[152,152,316]{2,1,0:T(8,128)(2,1)} %bitcast.22), custom_call_target="tpu_custom_call" | custom-call | bytes 45000000 | tf_op jit(solution)/shard_map/pallas_call | solution.py:180
  50.5 1.4 %collective-permute-start.1 = (bf16[288,152]{1,0:T(8,128)(2,1)S(1)}, bf16[288,152]{1,0:T(8,128)(2,1)S(1)}, u32[]{:S(2)}, u32[]{:S(2)}) collective-permute-start(bf16[288,152]{1,0:T(8,128)(2,1)S(1)} %constant_dynamic-update-slice_fusion), channel_id=1, source_target_pairs={{0,2},{1,3},{2,0},{3,1},{4,6},{5,7},{6,4},{7,5},{8,10},{9,11},{10,... | collective-permute-start | bytes 262664 | tf_op jit(solution)/shard_map/ppermute | solution.py:193
  51.9 0.6 collective-permute-start
  52.5 0.8 fusion.2.codes_ref
  53.3 0.9 reshape.28.coarse_ref
  54.2 0.5 collective-permute-done.1.g1
  54.8 0.1 copy-done.6
  54.8 0.1 copy-done.7
  55.0 0.4 copy-done.9
  55.4 0.7 copy-done.10
  56.1 71.2 %shard_map.119 = f32[152,256]{1,0:T(8,128)} custom-call(s32[40,16,128]{2,1,0:T(8,128)} %fusion.2.codes_ref, s32[40,8,256]{2,1,0:T(8,128)} %copy-done.2, s32[40,1,256]{2,1,0:T(1,128)} %reshape.49.plane_ref, bf16[40,160,2048]{2,1,0:T(8,128)(2,1)} %shard_map.118.w_ref, bf16[256,152]{1,0:T(8,128)(2,1)} %bitcast.25, bf16[288,152]{1,0:T(8,128)(2,1)} %copy-done.10, ...), custom_call_target="tpu_custom_call" | custom-call | flops 4322111488 | bytes 28000000 | tf_op jit(solution)/shard_map/pallas_call | solution.py:130
  (34 shorter events, 0.3 us)
Async XLA Ops:
  0.0 3.6 %copy-start = (bf16[8,152,152]{2,1,0:T(8,128)(2,1)S(1)}, bf16[8,152,152]{2,1,0:T(8,128)(2,1)}, u32[]{:S(2)}) copy-start(bf16[8,152,152]{2,1,0:T(8,128)(2,1)} %param.13) | copy-start | bytes 1108996
  2.4 50.9 %copy-start.1 = (bf16[152,256]{0,1:T(8,128)(2,1)}, bf16[152,256]{0,1:T(8,128)(2,1)S(1)}, u32[]{:S(2)}) copy-start(bf16[152,256]{0,1:T(8,128)(2,1)S(1)} %copy.20) | copy-start | bytes 233476
  3.9 50.9 %copy-start.3 = (bf16[152,32]{0,1:T(8,128)(2,1)}, bf16[152,32]{0,1:T(8,128)(2,1)S(1)}, u32[]{:S(2)}) copy-start(bf16[152,32]{0,1:T(8,128)(2,1)S(1)} %fusion) | copy-start | bytes 29188
  4.6 45.9 %collective-permute-start.6 = (bf16[288,152]{1,0:T(8,128)(2,1)S(1)}, bf16[288,152]{1,0:T(8,128)(2,1)S(1)}, u32[]{:S(2)}, u32[]{:S(2)}) collective-permute-start(bf16[288,152]{1,0:T(8,128)(2,1)S(1)} %constant_dynamic-update-slice_fusion), channel_id=1, source_target_pairs={{0,64},{32,96},{64,0},{96,32},{1,65},{33,97},{65,1},{97,33},{2,66}... | collective-permute-start | bytes 262664 | tf_op jit(solution)/shard_map/ppermute | solution.py:193
  9.1 42.8 %collective-permute-start.5 = (bf16[288,152]{1,0:T(8,128)(2,1)S(1)}, bf16[288,152]{1,0:T(8,128)(2,1)S(1)}, u32[]{:S(2)}, u32[]{:S(2)}) collective-permute-start(bf16[288,152]{1,0:T(8,128)(2,1)S(1)} %constant_dynamic-update-slice_fusion), channel_id=1, source_target_pairs={{0,32},{32,0},{64,96},{96,64},{1,33},{33,1},{65,97},{97,65},{2,34}... | collective-permute-start | bytes 262664 | tf_op jit(solution)/shard_map/ppermute | solution.py:193
  9.8 44.4 %collective-permute-start.4 = (bf16[288,152]{1,0:T(8,128)(2,1)S(1)}, bf16[288,152]{1,0:T(8,128)(2,1)S(1)}, u32[]{:S(2)}, u32[]{:S(2)}) collective-permute-start(bf16[288,152]{1,0:T(8,128)(2,1)S(1)} %constant_dynamic-update-slice_fusion), channel_id=1, source_target_pairs={{0,16},{1,17},{2,18},{3,19},{4,20},{5,21},{6,22},{7,23},{8,24},{9,... | collective-permute-start | bytes 262664 | tf_op jit(solution)/shard_map/ppermute | solution.py:193
  12.5 41.7 %collective-permute-start.3 = (bf16[288,152]{1,0:T(8,128)(2,1)S(1)}, bf16[288,152]{1,0:T(8,128)(2,1)S(1)}, u32[]{:S(2)}, u32[]{:S(2)}) collective-permute-start(bf16[288,152]{1,0:T(8,128)(2,1)S(1)} %constant_dynamic-update-slice_fusion), channel_id=1, source_target_pairs={{0,8},{1,9},{2,10},{3,11},{4,12},{5,13},{6,14},{7,15},{8,0},{9,1},... | collective-permute-start | bytes 262664 | tf_op jit(solution)/shard_map/ppermute | solution.py:193
  12.9 41.4 %collective-permute-start.2 = (bf16[288,152]{1,0:T(8,128)(2,1)S(1)}, bf16[288,152]{1,0:T(8,128)(2,1)S(1)}, u32[]{:S(2)}, u32[]{:S(2)}) collective-permute-start(bf16[288,152]{1,0:T(8,128)(2,1)S(1)} %constant_dynamic-update-slice_fusion), channel_id=1, source_target_pairs={{0,4},{1,5},{2,6},{3,7},{4,0},{5,1},{6,2},{7,3},{8,12},{9,13},{10,... | collective-permute-start | bytes 262664 | tf_op jit(solution)/shard_map/ppermute | solution.py:193
  16.9 36.4 %all-to-all-start = ((bf16[128,4,152]{2,1,0:T(4,128)(2,1)}), bf16[128,4,152]{2,1,0:T(4,128)(2,1)S(1)}, u32[]{:S(2)}, u32[]{:S(2)}) async-start(bf16[128,4,152]{2,1,0:T(4,128)(2,1)} %broadcast_in_dim.34), calls=%async_computation | async-start | bytes 524288 | tf_op jit(solution)/shard_map/all_to_all | solution.py:229
  24.1 30.7 %copy-start.2 = (s32[40,8,256]{2,1,0:T(8,128)}, s32[40,8,256]{2,1,0:T(8,128)S(1)}, u32[]{:S(2)}) copy-start(s32[40,8,256]{2,1,0:T(8,128)S(1)} %pad_bitcast_fusion.lanes_ref) | copy-start | bytes 983044
  50.5 4.3 %copy-start.4 = (bf16[288,152]{1,0:T(8,128)(2,1)}, bf16[288,152]{1,0:T(8,128)(2,1)S(1)}, u32[]{:S(2)}) copy-start(bf16[288,152]{1,0:T(8,128)(2,1)S(1)} %collective-permute-done.6.g6) | copy-start | bytes 262660
  50.5 4.3 %collective-permute-start.1 = (bf16[288,152]{1,0:T(8,128)(2,1)S(1)}, bf16[288,152]{1,0:T(8,128)(2,1)S(1)}, u32[]{:S(2)}, u32[]{:S(2)}) collective-permute-start(bf16[288,152]{1,0:T(8,128)(2,1)S(1)} %constant_dynamic-update-slice_fusion), channel_id=1, source_target_pairs={{0,2},{1,3},{2,0},{3,1},{4,6},{5,7},{6,4},{7,5},{8,10},{9,11},{10,... | collective-permute-start | bytes 262664 | tf_op jit(solution)/shard_map/ppermute | solution.py:193
  51.9 2.9 %copy-start.5 = (bf16[288,152]{1,0:T(8,128)(2,1)}, bf16[288,152]{1,0:T(8,128)(2,1)S(1)}, u32[]{:S(2)}) copy-start(bf16[288,152]{1,0:T(8,128)(2,1)S(1)} %collective-permute-done.5.g5) | copy-start | bytes 262660
  51.9 2.9 %collective-permute-start = (bf16[288,152]{1,0:T(8,128)(2,1)S(1)}, bf16[288,152]{1,0:T(8,128)(2,1)S(1)}, u32[]{:S(2)}, u32[]{:S(2)}) collective-permute-start(bf16[288,152]{1,0:T(8,128)(2,1)S(1)} %constant_dynamic-update-slice_fusion), channel_id=1, source_target_pairs={{0,1},{1,0},{2,3},{3,2},{4,5},{5,4},{6,7},{7,6},{8,9},{9,8},{10,11... | collective-permute-start | bytes 262664 | tf_op jit(solution)/shard_map/ppermute | solution.py:193
  54.2 0.6 copy-start.6
  54.2 0.7 copy-start.7
  54.2 0.7 copy-start.8
  54.7 0.7 copy-start.9
  55.4 0.7 copy-start.10

commit v3 on v2

--- a/solution.py
+++ b/solution.py
@@ -7,7 +7,7 @@
 
 NOFF, P_SIZE = 316, 152
 BLOCK = 8
-COPIED = 5
+COPIED = 6
 NBLOCK = 40
 LEAVES, PARENTS, COARSE = 256, 32, 4
 ROWS = 296
@@ -18,9 +18,9 @@
 
 
 def main_kernel(codes_ref, lanes_ref, plane_ref, w_ref, own_ref, g0, g1, g2, g3, g4, g5, g6, pown_ref, coarse_ref,
-                down_ref, out_ref, table, columns, held, ptable, wbuf, c0, c1, p0, p1, acc, turned, wsem, csem):
+                down_ref, out_ref, table, columns, h0, h1, v0, v1, ptable, wbuf, c0, c1, p0, p1, acc, turned, wsem, csem):
     nit = NBLOCK // 2
-    codes, picks = (c0, c1), (p0, p1)
+    codes, picks, helds, wides = (c0, c1), (p0, p1), (h0, h1), (v0, v1)
 
     def wcopy(i):
         return pltpu.make_async_copy(w_ref.at[pl.ds(i * 2, 2)], wbuf.at[pl.ds(i * 2, 2)], wsem.at[i])
@@ -43,7 +43,8 @@
         flat[pl.ds(2 * base, n, stride=2), :] = wide[:, :128]
         flat[pl.ds(2 * base + 1, n, stride=2), :] = wide[:, 128:]
 
-    held[...] = jnp.zeros_like(held)
+    for ref in (h0, h1, p1, v1):
+        ref[...] = jnp.zeros_like(ref)
     for b, g in enumerate((own_ref, g0, g1, g2, g3, g4, g5, g6)):
         wide = widened(g[0:LEAVES, :])
         fill(LEAVES * b, wide)
@@ -67,41 +68,42 @@
         hot = lax.broadcasted_iota(jnp.int32, (depth, column.shape[1]), 0) == column - base
         return jnp.where(hot, 1.0, 0.0).astype(jnp.bfloat16)
 
+    def few(slot, o, h):
+        at = COPIED * LEAVES + o * 8
+        lines = picks[slot].reshape((COPIED * LEAVES + BLOCK * 8) * 2, 128)
+        return [wides[slot][o * PARENTS:(o + 1) * PARENTS, h * 128:h * 128 + 128], lines[pl.ds(2 * at + h, 8, stride=2), :]]
+
+    def multiply(b, slot, o):
+        if o < COPIED:
+            lines = picks[slot].reshape((COPIED * LEAVES + BLOCK * 8) * 2, 128)
+            x = [jnp.concatenate([lines[pl.ds(o * LEAVES * 2 + h, LEAVES, stride=2), :]] + few(slot, o, h), axis=0).astype(jnp.bfloat16) for h in range(2)]
+            acc[...] += lax.dot_general(jnp.concatenate(x, axis=1), wbuf[b, :, o * 256:(o + 1) * 256], NT, preferred_element_type=jnp.float32)
+        elif o == COPIED:
+            turned[...] += jnp.dot(wbuf[b, :, COPIED * 256:BLOCK * 256], helds[slot][...].astype(jnp.bfloat16), preferred_element_type=jnp.float32)
+        else:
+            x = [jnp.concatenate(few(slot, o, h), axis=0).astype(jnp.bfloat16) for o in range(COPIED, BLOCK) for h in range(2)]
+            acc[LEAVES:ROWS, :] += lax.dot_general(jnp.concatenate(x, axis=1), wbuf[b, :, COPIED * 256:BLOCK * 256], NT, preferred_element_type=jnp.float32)
+
+    pieces = [(o, k) for o in range(BLOCK - COPIED) for k in range(2048 // PIECE)]
+    share = COPIED * LEAVES // len(pieces)
+
     def block(b, slot):
-        pieces = [(o, k) for o in range(BLOCK - COPIED) for k in range(2048 // PIECE)]
-        share = COPIED * LEAVES // len(pieces)
-        wide = jnp.dot(ptable[...], chosen(plane_ref[b], 256, 0), preferred_element_type=jnp.float32).T
-        lines = picks[slot].reshape((COPIED * LEAVES + BLOCK * 8) * 2, 128)
-        for o in range(BLOCK):
-            for t in range(COARSE):
-                pick_row = flat[pl.ds(codes[slot][(COPIED * LEAVES) // 128, o * COARSE + t], 2), :]
-                picks[slot][COPIED * LEAVES + o * 8 + t] = pick_row
         for n, (o, k) in enumerate(pieces):
             @pl.when(b >= 0)
             def _():
                 hot = chosen(lanes_ref[b, COPIED + o:COPIED + o + 1, :], PIECE, k * PIECE)
                 found = jnp.dot(columns[:, k * PIECE:(k + 1) * PIECE], hot, preferred_element_type=jnp.float32)
+                if n < COPIED + 2:
+                    multiply(jnp.maximum(b - 1, 0), 1 - slot, n)
+                copy_rows(slot, n * share, COPIED * LEAVES if n == len(pieces) - 1 else (n + 1) * share)
                 rows = slice(o * 256, o * 256 + PADDED)
-                copy_rows(slot, n * share, COPIED * LEAVES if n == len(pieces) - 1 else (n + 1) * share)
-                held[rows, :] = found if k == 0 else held[rows, :] + found
-
-        def few(o, h):
-            at = COPIED * LEAVES + o * 8
-            return [wide[o * PARENTS:(o + 1) * PARENTS, h * 128:h * 128 + 128], lines[pl.ds(2 * at + h, 8, stride=2), :]]
-
-        tail = wbuf[b, :, COPIED * 256:BLOCK * 256]
-        turned[...] += jnp.dot(tail, held[...].astype(jnp.bfloat16), preferred_element_type=jnp.float32)
-        rest = jnp.concatenate([jnp.concatenate(few(o, h), axis=0).astype(jnp.bfloat16) for o in range(COPIED, BLOCK) for h in range(2)], axis=1)
-        acc[LEAVES:ROWS, :] += lax.dot_general(rest, tail, NT, preferred_element_type=jnp.float32)
-        x = jnp.concatenate(
-            [
-                jnp.concatenate([lines[pl.ds(o * LEAVES * 2 + h, LEAVES, stride=2), :]] + few(o, h), axis=0).astype(jnp.bfloat16)
-                for o in range(COPIED)
-                for h in range(2)
-            ],
-            axis=1,
-        )
-        acc[...] += lax.dot_general(x, wbuf[b, :, 0:COPIED * 256], NT, preferred_element_type=jnp.float32)
+                helds[slot][rows, :] = found if k == 0 else helds[slot][rows, :] + found
+                if n == len(pieces) - 1:
+                    wides[slot][...] = jnp.dot(ptable[...], chosen(plane_ref[b], 256, 0), preferred_element_type=jnp.float32).T
+                    for m in range(BLOCK):
+                        for t in range(COARSE):
+                            code = codes[slot][(COPIED * LEAVES) // 128, m * COARSE + t]
+                            picks[slot][COPIED * LEAVES + m * 8 + t] = flat[pl.ds(code, 2), :]
 
     def body(i, _):
         wcopy(i).wait()
@@ -114,6 +116,8 @@
         return 0
 
     lax.fori_loop(0, nit, body, 0)
+    for n in range(COPIED + 2):
+        multiply(NBLOCK - 1, 1, n)
 
     coarse_local = acc[288:296, 0:P_SIZE].astype(jnp.bfloat16)
     spread = [lax.dot_general(coarse_local, down_ref[c], NT, preferred_element_type=jnp.float32)[0:4] for c in range(8)]
@@ -135,7 +139,8 @@
         scratch_shapes=[
             pltpu.VMEM((TABLE, 2, 128), jnp.float32),
             pltpu.VMEM((PADDED, 2048), jnp.bfloat16),
-            pltpu.VMEM(((BLOCK - COPIED) * 256, LEAVES), jnp.float32),
+            pltpu.VMEM(((BLOCK - COPIED) * 256, LEAVES), jnp.float32), pltpu.VMEM(((BLOCK - COPIED) * 256, LEAVES), jnp.float32),
+            pltpu.VMEM((256, 256), jnp.float32), pltpu.VMEM((256, 256), jnp.float32),
             pltpu.VMEM((256, 256), jnp.bfloat16),
             pltpu.VMEM((NBLOCK, PADDED, BLOCK * 256), jnp.bfloat16),
             pltpu.SMEM((16, 128), jnp.int32), pltpu.SMEM((16, 128), jnp.int32),

time: 129 us -> 121 us (0.938)
  Pallas kernels: 94.8 us -> 86.6 us
    pallas_call x1, Pallas kernels: 71.2 us -> 63 us  [main_call(): pl.pallas_call(main_kernel, in_specs=[anyspec, vm, vm, anyspec] + [vm] *...]
  transfers between devices with their start and end apart: 8 -> 8, of which waited for: 1 -> 1; matrix products, arithmetic and copies ran while one was open for 5% -> 6% of each run, Pallas kernels for 19% -> 20%
where the time goes in v3:
time: 121 us; the launch traced here: 119 us
  Pallas kernels  86.6 us (72%)
  starting transfers between devices  19.3 us (16%)
  local copies, waits for them, and re-layouts  7.06 us (6%)
  other arithmetic  4.92 us (4%)
    pallas_call x1, Pallas kernels, main_call(): pl.pallas_call(main_kernel, in_specs=[anyspec, vm, vm, anyspec] + [vm] *...  63 us
    pallas_call x1, Pallas kernels, relay(): pl.pallas_call(relay_kernel, grid=(PADDED // PBLOCK,), in_specs=[pl.Block...  23.6 us
    ppermute x7, starting transfers between devices, swapped(): lax.ppermute(array, axis, [(i, i ^ 1 << distance) for i in range(lax.axis...  13.2 us
    all_to_all x1, starting transfers between devices, shards(): lax.all_to_all(spread, ('gx', 'gy'), 0, 0, tiled=True).reshape(512, P_SIZE)  6.03 us
    unnamed x26, local copies, waits for them, and re-layouts  2.56 us
  transfers between devices with their start and end apart: 8, of which 1 were waited for; matrix products, arithmetic and copies ran while one was open for 6% of the time, Pallas kernels for 20%

profile of v3, /device:TPU:1, one launch (start us, length us, event | category | flops | bytes accessed | tf_op | source)
XLA Modules:
  0.0 119.1 jit_solution(6539207120512190857)
XLA Ops:
  0.0 0.7 compare_select_fusion.4
  0.7 0.7 compare_select_fusion.3
  1.4 1.0 copy.20
  2.4 1.2 gather_fusion
  3.6 0.3 fusion
  3.9 0.7 gather_fusion.1
  4.6 4.5 %collective-permute-start.6 = (bf16[288,152]{1,0:T(8,128)(2,1)S(1)}, bf16[288,152]{1,0:T(8,128)(2,1)S(1)}, u32[]{:S(2)}, u32[]{:S(2)}) collective-permute-start(bf16[288,152]{1,0:T(8,128)(2,1)S(1)} %constant_dynamic-update-slice_fusion), channel_id=1, source_target_pairs={{0,64},{32,96},{64,0},{96,32},{1,65},{33,97},{65,1},{97,33},{2,66}... | collective-permute-start | bytes 262664 | tf_op jit(solution)/shard_map/ppermute | solution.py:198
  9.1 0.7 collective-permute-start.5
  9.8 2.7 %collective-permute-start.4 = (bf16[288,152]{1,0:T(8,128)(2,1)S(1)}, bf16[288,152]{1,0:T(8,128)(2,1)S(1)}, u32[]{:S(2)}, u32[]{:S(2)}) collective-permute-start(bf16[288,152]{1,0:T(8,128)(2,1)S(1)} %constant_dynamic-update-slice_fusion), channel_id=1, source_target_pairs={{0,16},{1,17},{2,18},{3,19},{4,20},{5,21},{6,22},{7,23},{8,24},{9,... | collective-permute-start | bytes 262664 | tf_op jit(solution)/shard_map/ppermute | solution.py:198
  12.5 0.3 collective-permute-start.3
  12.9 2.9 %collective-permute-start.2 = (bf16[288,152]{1,0:T(8,128)(2,1)S(1)}, bf16[288,152]{1,0:T(8,128)(2,1)S(1)}, u32[]{:S(2)}, u32[]{:S(2)}) collective-permute-start(bf16[288,152]{1,0:T(8,128)(2,1)S(1)} %constant_dynamic-update-slice_fusion), channel_id=1, source_target_pairs={{0,4},{1,5},{2,6},{3,7},{4,0},{5,1},{6,2},{7,3},{8,12},{9,13},{10,... | collective-permute-start | bytes 262664 | tf_op jit(solution)/shard_map/ppermute | solution.py:198
  15.8 0.2 fusion.1
  16.0 0.8 broadcast_in_dim.34
  16.9 6.0 %all-to-all-start = ((bf16[128,4,152]{2,1,0:T(4,128)(2,1)}), bf16[128,4,152]{2,1,0:T(4,128)(2,1)S(1)}, u32[]{:S(2)}, u32[]{:S(2)}) async-start(bf16[128,4,152]{2,1,0:T(4,128)(2,1)} %broadcast_in_dim.34), calls=%async_computation | async-start | bytes 524288 | tf_op jit(solution)/shard_map/all_to_all | solution.py:234
  22.9 1.1 compare_select_fusion.1
  24.2 0.9 compare_select_fusion.2
  25.0 0.7 add_select_fusion
  25.7 0.1 copy.24
  25.9 0.7 reshape.49.plane_ref
  26.6 0.1 copy.23
  26.8 0.1 reshape.24
  26.9 23.6 %shard_map.118.w_ref = bf16[40,160,2048]{2,1,0:T(8,128)(2,1)} custom-call(bf16[152,152,316]{2,1,0:T(8,128)(2,1)} %bitcast.22), custom_call_target="tpu_custom_call" | custom-call | bytes 45000000 | tf_op jit(solution)/shard_map/pallas_call | solution.py:185
  50.5 1.4 %collective-permute-start.1 = (bf16[288,152]{1,0:T(8,128)(2,1)S(1)}, bf16[288,152]{1,0:T(8,128)(2,1)S(1)}, u32[]{:S(2)}, u32[]{:S(2)}) collective-permute-start(bf16[288,152]{1,0:T(8,128)(2,1)S(1)} %constant_dynamic-update-slice_fusion), channel_id=1, source_target_pairs={{0,2},{1,3},{2,0},{3,1},{4,6},{5,7},{6,4},{7,5},{8,10},{9,11},{10,... | collective-permute-start | bytes 262664 | tf_op jit(solution)/shard_map/ppermute | solution.py:198
  51.9 0.6 collective-permute-start
  52.5 0.8 fusion.2.codes_ref
  53.3 0.9 reshape.28.coarse_ref
  54.2 0.5 collective-permute-done.1.g1
  54.8 0.1 copy-done.6
  54.8 0.1 copy-done.7
  55.0 0.4 copy-done.9
  55.4 0.7 copy-done.10
  56.1 63.0 %shard_map.119 = f32[152,256]{1,0:T(8,128)} custom-call(s32[40,16,128]{2,1,0:T(8,128)} %fusion.2.codes_ref, s32[40,8,256]{2,1,0:T(8,128)} %copy-done.2, s32[40,1,256]{2,1,0:T(1,128)} %reshape.49.plane_ref, bf16[40,160,2048]{2,1,0:T(8,128)(2,1)} %shard_map.118.w_ref, bf16[256,152]{1,0:T(8,128)(2,1)} %bitcast.25, bf16[288,152]{1,0:T(8,128)(2,1)} %copy-done.10, ...), custom_call_target="tpu_custom_call" | custom-call | flops 4322111488 | bytes 28000000 | tf_op jit(solution)/shard_map/pallas_call | solution.py:134
  (34 shorter events, 0.3 us)
Async XLA Ops:
  0.0 3.6 %copy-start = (bf16[8,152,152]{2,1,0:T(8,128)(2,1)S(1)}, bf16[8,152,152]{2,1,0:T(8,128)(2,1)}, u32[]{:S(2)}) copy-start(bf16[8,152,152]{2,1,0:T(8,128)(2,1)} %param.13) | copy-start | bytes 1108996
  2.4 50.9 %copy-start.1 = (bf16[152,256]{0,1:T(8,128)(2,1)}, bf16[152,256]{0,1:T(8,128)(2,1)S(1)}, u32[]{:S(2)}) copy-start(bf16[152,256]{0,1:T(8,128)(2,1)S(1)} %copy.20) | copy-start | bytes 233476
  3.9 50.9 %copy-start.3 = (bf16[152,32]{0,1:T(8,128)(2,1)}, bf16[152,32]{0,1:T(8,128)(2,1)S(1)}, u32[]{:S(2)}) copy-start(bf16[152,32]{0,1:T(8,128)(2,1)S(1)} %fusion) | copy-start | bytes 29188
  4.6 45.9 %collective-permute-start.6 = (bf16[288,152]{1,0:T(8,128)(2,1)S(1)}, bf16[288,152]{1,0:T(8,128)(2,1)S(1)}, u32[]{:S(2)}, u32[]{:S(2)}) collective-permute-start(bf16[288,152]{1,0:T(8,128)(2,1)S(1)} %constant_dynamic-update-slice_fusion), channel_id=1, source_target_pairs={{0,64},{32,96},{64,0},{96,32},{1,65},{33,97},{65,1},{97,33},{2,66}... | collective-permute-start | bytes 262664 | tf_op jit(solution)/shard_map/ppermute | solution.py:198
  9.1 42.8 %collective-permute-start.5 = (bf16[288,152]{1,0:T(8,128)(2,1)S(1)}, bf16[288,152]{1,0:T(8,128)(2,1)S(1)}, u32[]{:S(2)}, u32[]{:S(2)}) collective-permute-start(bf16[288,152]{1,0:T(8,128)(2,1)S(1)} %constant_dynamic-update-slice_fusion), channel_id=1, source_target_pairs={{0,32},{32,0},{64,96},{96,64},{1,33},{33,1},{65,97},{97,65},{2,34}... | collective-permute-start | bytes 262664 | tf_op jit(solution)/shard_map/ppermute | solution.py:198
  9.8 44.4 %collective-permute-start.4 = (bf16[288,152]{1,0:T(8,128)(2,1)S(1)}, bf16[288,152]{1,0:T(8,128)(2,1)S(1)}, u32[]{:S(2)}, u32[]{:S(2)}) collective-permute-start(bf16[288,152]{1,0:T(8,128)(2,1)S(1)} %constant_dynamic-update-slice_fusion), channel_id=1, source_target_pairs={{0,16},{1,17},{2,18},{3,19},{4,20},{5,21},{6,22},{7,23},{8,24},{9,... | collective-permute-start | bytes 262664 | tf_op jit(solution)/shard_map/ppermute | solution.py:198
  12.5 41.7 %collective-permute-start.3 = (bf16[288,152]{1,0:T(8,128)(2,1)S(1)}, bf16[288,152]{1,0:T(8,128)(2,1)S(1)}, u32[]{:S(2)}, u32[]{:S(2)}) collective-permute-start(bf16[288,152]{1,0:T(8,128)(2,1)S(1)} %constant_dynamic-update-slice_fusion), channel_id=1, source_target_pairs={{0,8},{1,9},{2,10},{3,11},{4,12},{5,13},{6,14},{7,15},{8,0},{9,1},... | collective-permute-start | bytes 262664 | tf_op jit(solution)/shard_map/ppermute | solution.py:198
  12.9 41.4 %collective-permute-start.2 = (bf16[288,152]{1,0:T(8,128)(2,1)S(1)}, bf16[288,152]{1,0:T(8,128)(2,1)S(1)}, u32[]{:S(2)}, u32[]{:S(2)}) collective-permute-start(bf16[288,152]{1,0:T(8,128)(2,1)S(1)} %constant_dynamic-update-slice_fusion), channel_id=1, source_target_pairs={{0,4},{1,5},{2,6},{3,7},{4,0},{5,1},{6,2},{7,3},{8,12},{9,13},{10,... | collective-permute-start | bytes 262664 | tf_op jit(solution)/shard_map/ppermute | solution.py:198
  16.9 36.4 %all-to-all-start = ((bf16[128,4,152]{2,1,0:T(4,128)(2,1)}), bf16[128,4,152]{2,1,0:T(4,128)(2,1)S(1)}, u32[]{:S(2)}, u32[]{:S(2)}) async-start(bf16[128,4,152]{2,1,0:T(4,128)(2,1)} %broadcast_in_dim.34), calls=%async_computation | async-start | bytes 524288 | tf_op jit(solution)/shard_map/all_to_all | solution.py:234
  24.1 30.7 %copy-start.2 = (s32[40,8,256]{2,1,0:T(8,128)}, s32[40,8,256]{2,1,0:T(8,128)S(1)}, u32[]{:S(2)}) copy-start(s32[40,8,256]{2,1,0:T(8,128)S(1)} %pad_bitcast_fusion.lanes_ref) | copy-start | bytes 983044
  50.5 4.3 %copy-start.4 = (bf16[288,152]{1,0:T(8,128)(2,1)}, bf16[288,152]{1,0:T(8,128)(2,1)S(1)}, u32[]{:S(2)}) copy-start(bf16[288,152]{1,0:T(8,128)(2,1)S(1)} %collective-permute-done.6.g6) | copy-start | bytes 262660
  50.5 4.3 %collective-permute-start.1 = (bf16[288,152]{1,0:T(8,128)(2,1)S(1)}, bf16[288,152]{1,0:T(8,128)(2,1)S(1)}, u32[]{:S(2)}, u32[]{:S(2)}) collective-permute-start(bf16[288,152]{1,0:T(8,128)(2,1)S(1)} %constant_dynamic-update-slice_fusion), channel_id=1, source_target_pairs={{0,2},{1,3},{2,0},{3,1},{4,6},{5,7},{6,4},{7,5},{8,10},{9,11},{10,... | collective-permute-start | bytes 262664 | tf_op jit(solution)/shard_map/ppermute | solution.py:198
  51.9 2.9 %copy-start.5 = (bf16[288,152]{1,0:T(8,128)(2,1)}, bf16[288,152]{1,0:T(8,128)(2,1)S(1)}, u32[]{:S(2)}) copy-start(bf16[288,152]{1,0:T(8,128)(2,1)S(1)} %collective-permute-done.5.g5) | copy-start | bytes 262660
  51.9 2.9 %collective-permute-start = (bf16[288,152]{1,0:T(8,128)(2,1)S(1)}, bf16[288,152]{1,0:T(8,128)(2,1)S(1)}, u32[]{:S(2)}, u32[]{:S(2)}) collective-permute-start(bf16[288,152]{1,0:T(8,128)(2,1)S(1)} %constant_dynamic-update-slice_fusion), channel_id=1, source_target_pairs={{0,1},{1,0},{2,3},{3,2},{4,5},{5,4},{6,7},{7,6},{8,9},{9,8},{10,11... | collective-permute-start | bytes 262664 | tf_op jit(solution)/shard_map/ppermute | solution.py:198
  54.2 0.6 copy-start.6
  54.2 0.7 copy-start.7
  54.2 0.7 copy-start.8
  54.7 0.7 copy-start.9
  55.4 0.7 copy-start.10

commit v4 on v3

--- a/solution.py
+++ b/solution.py
@@ -12,18 +12,21 @@
 LEAVES, PARENTS, COARSE = 256, 32, 4
 ROWS = 296
 TABLE, ZERO = 2568, 2560
-PADDED = 160
+PADDED, SPLIT = 160, 64
 PIECE = 512
 NT = (((1,), (1,)), ((), ()))
 
 
-def main_kernel(codes_ref, lanes_ref, plane_ref, w_ref, own_ref, g0, g1, g2, g3, g4, g5, g6, pown_ref, coarse_ref,
+def main_kernel(codes_ref, lanes_ref, plane_ref, wa_ref, wb_ref, own_ref, g0, g1, g2, g3, g4, g5, g6, pown_ref, coarse_ref,
                 down_ref, out_ref, table, columns, h0, h1, v0, v1, ptable, wbuf, c0, c1, p0, p1, acc, turned, wsem, csem):
     nit = NBLOCK // 2
     codes, picks, helds, wides = (c0, c1), (p0, p1), (h0, h1), (v0, v1)
 
-    def wcopy(i):
-        return pltpu.make_async_copy(w_ref.at[pl.ds(i * 2, 2)], wbuf.at[pl.ds(i * 2, 2)], wsem.at[i])
+    def wcopy(i, ref, half, first, last):
+        to = wbuf.at[pl.ds(i * 2, 2), pl.ds(first, last - first)]
+        return pltpu.make_async_copy(ref.at[pl.ds(i * 2, 2)], to, wsem.at[half, i])
+
+    parts = ((wa_ref, 0, 0, SPLIT), (wb_ref, 1, SPLIT, PADDED))
 
     def ccopy(b, slot):
         return pltpu.make_async_copy(codes_ref.at[b], codes[slot], csem.at[slot])
@@ -31,7 +34,8 @@
     ccopy(0, 0).start()
     ccopy(1, 1).start()
     for i in range(nit):
-        wcopy(i).start()
+        for part in parts:
+            wcopy(i, *part).start()
     flat = table.reshape(TABLE * 2, 128)
 
     def widened(rows):
@@ -43,8 +47,8 @@
         flat[pl.ds(2 * base, n, stride=2), :] = wide[:, :128]
         flat[pl.ds(2 * base + 1, n, stride=2), :] = wide[:, 128:]
 
-    for ref in (h0, h1, p1, v1):
-        ref[...] = jnp.zeros_like(ref)
+    for ref in (h0, h1, p1.reshape((COPIED * LEAVES + BLOCK * 8) * 2, 128), v1):
+        ref[...] = jnp.zeros(ref.shape, jnp.float32)
     for b, g in enumerate((own_ref, g0, g1, g2, g3, g4, g5, g6)):
         wide = widened(g[0:LEAVES, :])
         fill(LEAVES * b, wide)
@@ -106,7 +110,8 @@
                             picks[slot][COPIED * LEAVES + m * 8 + t] = flat[pl.ds(code, 2), :]
 
     def body(i, _):
-        wcopy(i).wait()
+        for part in parts:
+            wcopy(i, *part).wait()
         for slot in range(2):
             ccopy(2 * i + slot, slot).wait()
             block(2 * i + slot, slot)
@@ -127,13 +132,13 @@
     out_ref[...] = far.T + 4.0 * turned[0:P_SIZE, :]
 
 
-def main_call(codes, lanes, plane, w, own, ghosts, pown, coarse, down):
+def main_call(codes, lanes, plane, wa, wb, own, ghosts, pown, coarse, down):
     vm = pl.BlockSpec(memory_space=pltpu.VMEM)
     anyspec = pl.BlockSpec(memory_space=pl.ANY)
     picked = COPIED * LEAVES + BLOCK * 8
     return pl.pallas_call(
         main_kernel,
-        in_specs=[anyspec, vm, vm, anyspec] + [vm] * 11,
+        in_specs=[anyspec, vm, vm, anyspec, anyspec] + [vm] * 11,
         out_specs=vm,
         out_shape=jax.ShapeDtypeStruct((P_SIZE, LEAVES), jnp.float32),
         scratch_shapes=[
@@ -147,11 +152,11 @@
             pltpu.VMEM((picked, 2, 128), jnp.float32), pltpu.VMEM((picked, 2, 128), jnp.float32),
             pltpu.VMEM((ROWS, PADDED), jnp.float32),
             pltpu.VMEM((PADDED, LEAVES), jnp.float32),
-            pltpu.SemaphoreType.DMA((NBLOCK // 2,)), pltpu.SemaphoreType.DMA((2,)),
+            pltpu.SemaphoreType.DMA((2, NBLOCK // 2)), pltpu.SemaphoreType.DMA((2,)),
         ],
         compiler_params=pltpu.CompilerParams(vmem_limit_bytes=58 << 20),
         cost_estimate=pl.CostEstimate(flops=2 * 296 * 48032 * 152, bytes_accessed=28_000_000, transcendentals=0),
-    )(codes, lanes, plane, w, own, *ghosts, pown, coarse, down)
+    )(codes, lanes, plane, wa, wb, own, *ghosts, pown, coarse, down)
 
 
 def tables(codes_leaf, valid_leaf, codes_parent, valid_parent, codes_coarse, valid_coarse):
@@ -165,33 +170,52 @@
     codes = 2 * jnp.concatenate([jnp.where(rows < 0, ZERO, rows), coarse], axis=1)
     return codes, lanes, plane
 
-PBLOCK, STRIDE = 16, 328
-
-
-def relay_kernel(f_ref, o_ref, low, high):
-    for p in range(PBLOCK):
-        wide = jnp.concatenate([f_ref[p].astype(jnp.float32), jnp.zeros((256 - P_SIZE, NOFF), jnp.float32)], axis=0)
-        turned = wide.T
-        low[p * STRIDE:p * STRIDE + NOFF, :] = turned[:, :128]
-        high[p * STRIDE:p * STRIDE + NOFF, :] = turned[:, 128:]
-    for o in range(NOFF):
-        at = (o % BLOCK) * 256
-        o_ref[o // BLOCK, :, at:at + 128] = low[pl.ds(o, PBLOCK, stride=STRIDE), :].astype(jnp.bfloat16)
-        o_ref[o // BLOCK, :, at + 128:at + 256] = high[pl.ds(o, PBLOCK, stride=STRIDE), :].astype(jnp.bfloat16)
+
+PBLOCK, STRIDE = 32, 136
+
+
+def relay_kernel(f_ref, *refs):
+    o_ref, halves = refs[-7], refs[-6:]
+
+    def turn(k, p):
+        first, last = k * 128, min(k * 128 + 128, NOFF)
+        wide = f_ref[p, :, first:last].astype(jnp.float32)
+        wide = jnp.concatenate([wide, jnp.zeros((256 - P_SIZE, last - first), jnp.float32)], axis=0).T
+        for h in range(2):
+            halves[2 * k + h][p * STRIDE:p * STRIDE + last - first, :] = wide[:, h * 128:h * 128 + 128]
+
+    def give(o):
+        for h in range(2):
+            lane = (o % BLOCK) * 256 + h * 128
+            rows = halves[2 * (o // 128) + h][pl.ds(o % 128, PBLOCK, stride=STRIDE), :]
+            o_ref[o // BLOCK, :, lane:lane + 128] = rows.astype(jnp.bfloat16)
+
+    always = pl.program_id(0) >= 0
+    for k in range(4):
+        for quarter in range(4):
+            @pl.when(always)
+            def _():
+                if k < 3:
+                    for p in range(quarter * PBLOCK // 4, (quarter + 1) * PBLOCK // 4):
+                        turn(k, p)
+                if k > 0:
+                    for o in range((k - 1) * 128 + quarter * 32, min((k - 1) * 128 + quarter * 32 + 32, NOFF)):
+                        give(o)
     o_ref[NBLOCK - 1, :, (NOFF % BLOCK) * 256:] = jnp.zeros((PBLOCK, (BLOCK - NOFF % BLOCK) * 256), jnp.bfloat16)
 
 
-def relay(far):
+def relay(far, first, last, after):
+    start, steps = first // PBLOCK, (last - first) // PBLOCK
     return pl.pallas_call(
         relay_kernel,
-        grid=(PADDED // PBLOCK,),
-        in_specs=[pl.BlockSpec((PBLOCK, P_SIZE, NOFF), lambda i: (i, 0, 0))],
+        grid=(steps,),
+        in_specs=[pl.BlockSpec((PBLOCK, P_SIZE, NOFF), lambda i: (i + start, 0, 0))] + [pl.BlockSpec(memory_space=pl.ANY)] * len(after),
         out_specs=pl.BlockSpec((NBLOCK, PBLOCK, BLOCK * 256), lambda i: (0, i, 0)),
-        out_shape=jax.ShapeDtypeStruct((NBLOCK, PADDED, BLOCK * 256), jnp.bfloat16),
-        scratch_shapes=[pltpu.VMEM((STRIDE * PBLOCK, 128), jnp.float32)] * 2,
+        out_shape=jax.ShapeDtypeStruct((NBLOCK, last - first, BLOCK * 256), jnp.bfloat16),
+        scratch_shapes=[pltpu.VMEM((STRIDE * PBLOCK, 128), jnp.float32)] * 6,
         compiler_params=pltpu.CompilerParams(vmem_limit_bytes=58 << 20),
-        cost_estimate=pl.CostEstimate(flops=0, bytes_accessed=45_000_000, transcendentals=0),
-    )(jnp.transpose(far, (1, 2, 0)))
+        cost_estimate=pl.CostEstimate(flops=0, bytes_accessed=9_000_000 * steps, transcendentals=0),
+    )(jnp.transpose(far, (1, 2, 0)), *after)
 
 
 def swapped(array, axis, distance):
@@ -232,8 +256,10 @@
     ghosts = [swapped(outgoing, "gy", b) for b in range(5)] + [swapped(outgoing, "gx", b) for b in range(2)]
     spread = jnp.broadcast_to(coarse_mult[None], (128, 4, P_SIZE))
     coarse_all = lax.all_to_all(spread, ("gx", "gy"), 0, 0, tiled=True).reshape(512, P_SIZE)
+    first = relay(far_matrices, 0, SPLIT, [])
+    second = relay(far_matrices, SPLIT, PADDED, ghosts[5:7])
     codes, lanes, plane = tables(codes_leaf, valid_leaf, codes_parent, valid_parent, codes_coarse, valid_coarse)
-    return main_call(codes, lanes, plane, relay(far_matrices), own, ghosts, parent_own, coarse_all, down_matrices)
+    return main_call(codes, lanes, plane, first, second, own, ghosts, parent_own, coarse_all, down_matrices)
 
 
 def solution(mesh):

time: 121 us -> 121 us (level); the launches traced: 119 us -> 121 us
  Pallas kernels: 86.6 us -> 88.4 us
    pallas_call x2 -> x3, Pallas kernels: 86.6 us -> 88.4 us  [the longest x1 63.2 us: main_call(): pl.pallas_call(main_kernel, in_specs=[anyspec, vm, vm, anyspec, anyspec]...]
  transfers between devices with their start and end apart: 8 -> 8, of which waited for: 1 -> 0; matrix products, arithmetic and copies ran while one was open for 6% -> 6% of each run, Pallas kernels for 20% -> 21%
where the time goes in v4:
time: 121 us
  Pallas kernels  88.4 us (73%)
  starting transfers between devices  19.4 us (16%)
  local copies, waits for them, and re-layouts  7.19 us (6%)
  other arithmetic  4.92 us (4%)
    pallas_call x1, Pallas kernels, main_call(): pl.pallas_call(main_kernel, in_specs=[anyspec, vm, vm, anyspec, anyspec]...  63.2 us
    pallas_call x2, Pallas kernels, relay(): pl.pallas_call(relay_kernel, grid=(steps,), in_specs=[pl.BlockSpec((PBLOC...  25.3 us
    ppermute x7, starting transfers between devices, swapped(): lax.ppermute(array, axis, [(i, i ^ 1 << distance) for i in range(lax.axis...  13.3 us
    all_to_all x1, starting transfers between devices, shards(): lax.all_to_all(spread, ('gx', 'gy'), 0, 0, tiled=True).reshape(512, P_SIZE)  6.04 us
    unnamed x26, local copies, waits for them, and re-layouts  2.7 us
  transfers between devices with their start and end apart: 8, of which 0 were waited for; matrix products, arithmetic and copies ran while one was open for 6% of the time, Pallas kernels for 21%

profile of v4, /device:TPU:1, one launch (start us, length us, event | category | flops | bytes accessed | tf_op | source)
XLA Modules:
  0.0 120.8 jit_solution(2879545681721726806)
XLA Ops:
  0.0 0.7 compare_select_fusion.4
  0.7 0.7 compare_select_fusion.3
  1.4 1.0 copy.20
  2.4 1.2 gather_fusion
  3.6 0.3 fusion
  3.9 0.7 gather_fusion.1
  4.6 3.7 %collective-permute-start.6 = (bf16[288,152]{1,0:T(8,128)(2,1)S(1)}, bf16[288,152]{1,0:T(8,128)(2,1)S(1)}, u32[]{:S(2)}, u32[]{:S(2)}) collective-permute-start(bf16[288,152]{1,0:T(8,128)(2,1)S(1)} %constant_dynamic-update-slice_fusion), channel_id=1, source_target_pairs={{0,16},{1,17},{2,18},{3,19},{4,20},{5,21},{6,22},{7,23},{8,24},{9,... | collective-permute-start | bytes 262664 | tf_op jit(solution)/shard_map/ppermute | solution.py:222
  8.2 0.3 collective-permute-start.5
  8.5 2.9 %collective-permute-start.4 = (bf16[288,152]{1,0:T(8,128)(2,1)S(1)}, bf16[288,152]{1,0:T(8,128)(2,1)S(1)}, u32[]{:S(2)}, u32[]{:S(2)}) collective-permute-start(bf16[288,152]{1,0:T(8,128)(2,1)S(1)} %constant_dynamic-update-slice_fusion), channel_id=1, source_target_pairs={{0,4},{1,5},{2,6},{3,7},{4,0},{5,1},{6,2},{7,3},{8,12},{9,13},{10,... | collective-permute-start | bytes 262664 | tf_op jit(solution)/shard_map/ppermute | solution.py:222
  11.4 3.6 %collective-permute-start.1 = (bf16[288,152]{1,0:T(8,128)(2,1)S(1)}, bf16[288,152]{1,0:T(8,128)(2,1)S(1)}, u32[]{:S(2)}, u32[]{:S(2)}) collective-permute-start(bf16[288,152]{1,0:T(8,128)(2,1)S(1)} %constant_dynamic-update-slice_fusion), channel_id=1, source_target_pairs={{0,64},{32,96},{64,0},{96,32},{1,65},{33,97},{65,1},{97,33},{2,66}... | collective-permute-start | bytes 262664 | tf_op jit(solution)/shard_map/ppermute | solution.py:222
  15.0 0.7 collective-permute-start
  15.8 0.2 fusion.1
  16.0 0.8 broadcast_in_dim.34
  16.9 6.0 %all-to-all-start = ((bf16[128,4,152]{2,1,0:T(4,128)(2,1)}), bf16[128,4,152]{2,1,0:T(4,128)(2,1)S(1)}, u32[]{:S(2)}, u32[]{:S(2)}) async-start(bf16[128,4,152]{2,1,0:T(4,128)(2,1)} %broadcast_in_dim.34), calls=%async_computation | async-start | bytes 524288 | tf_op jit(solution)/shard_map/all_to_all | solution.py:258
  22.9 1.1 compare_select_fusion.1
  24.2 0.9 compare_select_fusion.2
  25.0 0.7 add_select_fusion
  25.7 0.1 copy.24
  25.9 0.7 reshape.49.plane_ref
  26.6 0.1 copy.23
  26.8 0.1 reshape.24
  26.9 10.8 %shard_map.118.wa_ref = bf16[40,64,2048]{2,1,0:T(8,128)(2,1)} custom-call(bf16[152,152,316]{2,1,0:T(8,128)(2,1)} %bitcast.22), custom_call_target="tpu_custom_call" | custom-call | bytes 18000000 | tf_op jit(solution)/shard_map/pallas_call | solution.py:209
  37.7 1.5 %collective-permute-start.3 = (bf16[288,152]{1,0:T(8,128)(2,1)S(1)}, bf16[288,152]{1,0:T(8,128)(2,1)S(1)}, u32[]{:S(2)}, u32[]{:S(2)}) collective-permute-start(bf16[288,152]{1,0:T(8,128)(2,1)S(1)} %constant_dynamic-update-slice_fusion), channel_id=1, source_target_pairs={{0,2},{1,3},{2,0},{3,1},{4,6},{5,7},{6,4},{7,5},{8,10},{9,11},{10,... | collective-permute-start | bytes 262664 | tf_op jit(solution)/shard_map/ppermute | solution.py:222
  39.1 0.6 collective-permute-start.2
  39.8 0.8 fusion.2.codes_ref
  40.6 14.5 %shard_map.119.wb_ref = bf16[40,96,2048]{2,1,0:T(8,128)(2,1)} custom-call(bf16[152,152,316]{2,1,0:T(8,128)(2,1)} %bitcast.23, bf16[288,152]{1,0:T(8,128)(2,1)} %copy-done.5, bf16[288,152]{1,0:T(8,128)(2,1)} %copy-done.4), custom_call_target="tpu_custom_call" | custom-call | bytes 27000000 | tf_op jit(solution)/shard_map/pallas_call | solution.py:209
  55.1 0.9 reshape.28.coarse_ref
  56.1 0.6 copy-done.6
  56.6 0.1 copy-done.7
  56.8 0.1 copy-done.9
  56.8 0.7 copy-done.10
  57.5 63.2 %shard_map.120 = f32[152,256]{1,0:T(8,128)} custom-call(s32[40,16,128]{2,1,0:T(8,128)} %fusion.2.codes_ref, s32[40,8,256]{2,1,0:T(8,128)} %copy-done.2, s32[40,1,256]{2,1,0:T(1,128)} %reshape.49.plane_ref, bf16[40,64,2048]{2,1,0:T(8,128)(2,1)} %shard_map.118.wa_ref, bf16[40,96,2048]{2,1,0:T(8,128)(2,1)} %shard_map.119.wb_ref, bf16[256,152]{1,0:T(8,128)(2,1)} %bitcast.26, ...), custom_call_target="tpu_custom_call" | custom-call | flops 4322111488 | bytes 28000000 | tf_op jit(solution)/shard_map/pallas_call | solution.py:139
  (35 shorter events, 0.3 us)
Async XLA Ops:
  0.0 3.6 %copy-start = (bf16[8,152,152]{2,1,0:T(8,128)(2,1)S(1)}, bf16[8,152,152]{2,1,0:T(8,128)(2,1)}, u32[]{:S(2)}) copy-start(bf16[8,152,152]{2,1,0:T(8,128)(2,1)} %param.13) | copy-start | bytes 1108996
  2.4 35.2 %copy-start.1 = (bf16[152,256]{0,1:T(8,128)(2,1)}, bf16[152,256]{0,1:T(8,128)(2,1)S(1)}, u32[]{:S(2)}) copy-start(bf16[152,256]{0,1:T(8,128)(2,1)S(1)} %copy.20) | copy-start | bytes 233476
  3.9 33.8 %copy-start.3 = (bf16[152,32]{0,1:T(8,128)(2,1)}, bf16[152,32]{0,1:T(8,128)(2,1)S(1)}, u32[]{:S(2)}) copy-start(bf16[152,32]{0,1:T(8,128)(2,1)S(1)} %fusion) | copy-start | bytes 29188
  4.6 51.4 %collective-permute-start.6 = (bf16[288,152]{1,0:T(8,128)(2,1)S(1)}, bf16[288,152]{1,0:T(8,128)(2,1)S(1)}, u32[]{:S(2)}, u32[]{:S(2)}) collective-permute-start(bf16[288,152]{1,0:T(8,128)(2,1)S(1)} %constant_dynamic-update-slice_fusion), channel_id=1, source_target_pairs={{0,16},{1,17},{2,18},{3,19},{4,20},{5,21},{6,22},{7,23},{8,24},{9,... | collective-permute-start | bytes 262664 | tf_op jit(solution)/shard_map/ppermute | solution.py:222
  8.2 47.8 %collective-permute-start.5 = (bf16[288,152]{1,0:T(8,128)(2,1)S(1)}, bf16[288,152]{1,0:T(8,128)(2,1)S(1)}, u32[]{:S(2)}, u32[]{:S(2)}) collective-permute-start(bf16[288,152]{1,0:T(8,128)(2,1)S(1)} %constant_dynamic-update-slice_fusion), channel_id=1, source_target_pairs={{0,8},{1,9},{2,10},{3,11},{4,12},{5,13},{6,14},{7,15},{8,0},{9,1},... | collective-permute-start | bytes 262664 | tf_op jit(solution)/shard_map/ppermute | solution.py:222
  8.5 47.5 %collective-permute-start.4 = (bf16[288,152]{1,0:T(8,128)(2,1)S(1)}, bf16[288,152]{1,0:T(8,128)(2,1)S(1)}, u32[]{:S(2)}, u32[]{:S(2)}) collective-permute-start(bf16[288,152]{1,0:T(8,128)(2,1)S(1)} %constant_dynamic-update-slice_fusion), channel_id=1, source_target_pairs={{0,4},{1,5},{2,6},{3,7},{4,0},{5,1},{6,2},{7,3},{8,12},{9,13},{10,... | collective-permute-start | bytes 262664 | tf_op jit(solution)/shard_map/ppermute | solution.py:222
  11.4 26.2 %collective-permute-start.1 = (bf16[288,152]{1,0:T(8,128)(2,1)S(1)}, bf16[288,152]{1,0:T(8,128)(2,1)S(1)}, u32[]{:S(2)}, u32[]{:S(2)}) collective-permute-start(bf16[288,152]{1,0:T(8,128)(2,1)S(1)} %constant_dynamic-update-slice_fusion), channel_id=1, source_target_pairs={{0,64},{32,96},{64,0},{96,32},{1,65},{33,97},{65,1},{97,33},{2,66}... | collective-permute-start | bytes 262664 | tf_op jit(solution)/shard_map/ppermute | solution.py:222
  15.0 24.1 %collective-permute-start = (bf16[288,152]{1,0:T(8,128)(2,1)S(1)}, bf16[288,152]{1,0:T(8,128)(2,1)S(1)}, u32[]{:S(2)}, u32[]{:S(2)}) collective-permute-start(bf16[288,152]{1,0:T(8,128)(2,1)S(1)} %constant_dynamic-update-slice_fusion), channel_id=1, source_target_pairs={{0,32},{32,0},{64,96},{96,64},{1,33},{33,1},{65,97},{97,65},{2,34}... | collective-permute-start | bytes 262664 | tf_op jit(solution)/shard_map/ppermute | solution.py:222
  16.9 38.2 %all-to-all-start = ((bf16[128,4,152]{2,1,0:T(4,128)(2,1)}), bf16[128,4,152]{2,1,0:T(4,128)(2,1)S(1)}, u32[]{:S(2)}, u32[]{:S(2)}) async-start(bf16[128,4,152]{2,1,0:T(4,128)(2,1)} %broadcast_in_dim.34), calls=%async_computation | async-start | bytes 524288 | tf_op jit(solution)/shard_map/all_to_all | solution.py:258
  24.1 16.5 %copy-start.2 = (s32[40,8,256]{2,1,0:T(8,128)}, s32[40,8,256]{2,1,0:T(8,128)S(1)}, u32[]{:S(2)}) copy-start(s32[40,8,256]{2,1,0:T(8,128)S(1)} %pad_bitcast_fusion.lanes_ref) | copy-start | bytes 983044
  37.6 2.9 %copy-start.4 = (bf16[288,152]{1,0:T(8,128)(2,1)}, bf16[288,152]{1,0:T(8,128)(2,1)S(1)}, u32[]{:S(2)}) copy-start(bf16[288,152]{1,0:T(8,128)(2,1)S(1)} %collective-permute-done.1.refs_1_.g6) | copy-start | bytes 262660
  37.7 18.4 %collective-permute-start.3 = (bf16[288,152]{1,0:T(8,128)(2,1)S(1)}, bf16[288,152]{1,0:T(8,128)(2,1)S(1)}, u32[]{:S(2)}, u32[]{:S(2)}) collective-permute-start(bf16[288,152]{1,0:T(8,128)(2,1)S(1)} %constant_dynamic-update-slice_fusion), channel_id=1, source_target_pairs={{0,2},{1,3},{2,0},{3,1},{4,6},{5,7},{6,4},{7,5},{8,10},{9,11},{10,... | collective-permute-start | bytes 262664 | tf_op jit(solution)/shard_map/ppermute | solution.py:222
  39.1 1.4 %copy-start.5 = (bf16[288,152]{1,0:T(8,128)(2,1)}, bf16[288,152]{1,0:T(8,128)(2,1)S(1)}, u32[]{:S(2)}) copy-start(bf16[288,152]{1,0:T(8,128)(2,1)S(1)} %collective-permute-done.refs_0_.g5) | copy-start | bytes 262660
  39.1 16.9 %collective-permute-start.2 = (bf16[288,152]{1,0:T(8,128)(2,1)S(1)}, bf16[288,152]{1,0:T(8,128)(2,1)S(1)}, u32[]{:S(2)}, u32[]{:S(2)}) collective-permute-start(bf16[288,152]{1,0:T(8,128)(2,1)S(1)} %constant_dynamic-update-slice_fusion), channel_id=1, source_target_pairs={{0,1},{1,0},{2,3},{3,2},{4,5},{5,4},{6,7},{7,6},{8,9},{9,8},{10,11... | collective-permute-start | bytes 262664 | tf_op jit(solution)/shard_map/ppermute | solution.py:222
  56.0 0.6 copy-start.6
  56.0 0.7 copy-start.7
  56.0 0.7 copy-start.8
  56.0 0.8 copy-start.9
  56.8 0.7 copy-start.10

commit v5 on v4

--- a/solution.py
+++ b/solution.py
@@ -12,21 +12,18 @@
 LEAVES, PARENTS, COARSE = 256, 32, 4
 ROWS = 296
 TABLE, ZERO = 2568, 2560
-PADDED, SPLIT = 160, 64
+PADDED = 160
 PIECE = 512
 NT = (((1,), (1,)), ((), ()))
 
 
-def main_kernel(codes_ref, lanes_ref, plane_ref, wa_ref, wb_ref, own_ref, g0, g1, g2, g3, g4, g5, g6, pown_ref, coarse_ref,
+def main_kernel(codes_ref, lanes_ref, plane_ref, w_ref, own_ref, g0, g1, g2, g3, g4, g5, g6, pown_ref, coarse_ref,
                 down_ref, out_ref, table, columns, h0, h1, v0, v1, ptable, wbuf, c0, c1, p0, p1, acc, turned, wsem, csem):
     nit = NBLOCK // 2
     codes, picks, helds, wides = (c0, c1), (p0, p1), (h0, h1), (v0, v1)
 
-    def wcopy(i, ref, half, first, last):
-        to = wbuf.at[pl.ds(i * 2, 2), pl.ds(first, last - first)]
-        return pltpu.make_async_copy(ref.at[pl.ds(i * 2, 2)], to, wsem.at[half, i])
-
-    parts = ((wa_ref, 0, 0, SPLIT), (wb_ref, 1, SPLIT, PADDED))
+    def wcopy(i):
+        return pltpu.make_async_copy(w_ref.at[pl.ds(i * 2, 2)], wbuf.at[pl.ds(i * 2, 2)], wsem.at[i])
 
     def ccopy(b, slot):
         return pltpu.make_async_copy(codes_ref.at[b], codes[slot], csem.at[slot])
@@ -34,8 +31,7 @@
     ccopy(0, 0).start()
     ccopy(1, 1).start()
     for i in range(nit):
-        for part in parts:
-            wcopy(i, *part).start()
+        wcopy(i).start()
     flat = table.reshape(TABLE * 2, 128)
 
     def widened(rows):
@@ -110,8 +106,7 @@
                             picks[slot][COPIED * LEAVES + m * 8 + t] = flat[pl.ds(code, 2), :]
 
     def body(i, _):
-        for part in parts:
-            wcopy(i, *part).wait()
+        wcopy(i).wait()
         for slot in range(2):
             ccopy(2 * i + slot, slot).wait()
             block(2 * i + slot, slot)
@@ -132,13 +127,13 @@
     out_ref[...] = far.T + 4.0 * turned[0:P_SIZE, :]
 
 
-def main_call(codes, lanes, plane, wa, wb, own, ghosts, pown, coarse, down):
+def main_call(codes, lanes, plane, w, own, ghosts, pown, coarse, down):
     vm = pl.BlockSpec(memory_space=pltpu.VMEM)
     anyspec = pl.BlockSpec(memory_space=pl.ANY)
     picked = COPIED * LEAVES + BLOCK * 8
     return pl.pallas_call(
         main_kernel,
-        in_specs=[anyspec, vm, vm, anyspec, anyspec] + [vm] * 11,
+        in_specs=[anyspec, vm, vm, anyspec] + [vm] * 11,
         out_specs=vm,
         out_shape=jax.ShapeDtypeStruct((P_SIZE, LEAVES), jnp.float32),
         scratch_shapes=[
@@ -152,11 +147,11 @@
             pltpu.VMEM((picked, 2, 128), jnp.float32), pltpu.VMEM((picked, 2, 128), jnp.float32),
             pltpu.VMEM((ROWS, PADDED), jnp.float32),
             pltpu.VMEM((PADDED, LEAVES), jnp.float32),
-            pltpu.SemaphoreType.DMA((2, NBLOCK // 2)), pltpu.SemaphoreType.DMA((2,)),
+            pltpu.SemaphoreType.DMA((NBLOCK // 2,)), pltpu.SemaphoreType.DMA((2,)),
         ],
         compiler_params=pltpu.CompilerParams(vmem_limit_bytes=58 << 20),
         cost_estimate=pl.CostEstimate(flops=2 * 296 * 48032 * 152, bytes_accessed=28_000_000, transcendentals=0),
-    )(codes, lanes, plane, wa, wb, own, *ghosts, pown, coarse, down)
+    )(codes, lanes, plane, w, own, *ghosts, pown, coarse, down)
 
 
 def tables(codes_leaf, valid_leaf, codes_parent, valid_parent, codes_coarse, valid_coarse):
@@ -256,10 +251,9 @@
     ghosts = [swapped(outgoing, "gy", b) for b in range(5)] + [swapped(outgoing, "gx", b) for b in range(2)]
     spread = jnp.broadcast_to(coarse_mult[None], (128, 4, P_SIZE))
     coarse_all = lax.all_to_all(spread, ("gx", "gy"), 0, 0, tiled=True).reshape(512, P_SIZE)
-    first = relay(far_matrices, 0, SPLIT, [])
-    second = relay(far_matrices, SPLIT, PADDED, ghosts[5:7])
+    matrices = relay(far_matrices, 0, PADDED, ghosts[5:7])
     codes, lanes, plane = tables(codes_leaf, valid_leaf, codes_parent, valid_parent, codes_coarse, valid_coarse)
-    return main_call(codes, lanes, plane, first, second, own, ghosts, parent_own, coarse_all, down_matrices)
+    return main_call(codes, lanes, plane, matrices, own, ghosts, parent_own, coarse_all, down_matrices)
 
 
 def solution(mesh):

time: 121 us -> 117 us (0.967)
  Pallas kernels: 88.4 us -> 84.8 us
    pallas_call x2 -> x1, Pallas kernels: 25.3 us -> 21.7 us  [relay(): pl.pallas_call(relay_kernel, grid=(steps,), in_specs=[pl.BlockSpec((PBLOC...]
  transfers between devices with their start and end apart: 8 -> 8, of which waited for: 0 -> 0; matrix products, arithmetic and copies ran while one was open for 6% -> 6% of each run, Pallas kernels for 21% -> 19%
where the time goes in v5:
time: 117 us
  Pallas kernels  84.8 us (72%)
  starting transfers between devices  19.4 us (17%)
  local copies, waits for them, and re-layouts  7.17 us (6%)
  other arithmetic  4.92 us (4%)
    pallas_call x1, Pallas kernels, main_call(): pl.pallas_call(main_kernel, in_specs=[anyspec, vm, vm, anyspec] + [vm] *...  63.1 us
    pallas_call x1, Pallas kernels, relay(): pl.pallas_call(relay_kernel, grid=(steps,), in_specs=[pl.BlockSpec((PBLOC...  21.7 us
    ppermute x7, starting transfers between devices, swapped(): lax.ppermute(array, axis, [(i, i ^ 1 << distance) for i in range(lax.axis...  13.3 us
    all_to_all x1, starting transfers between devices, shards(): lax.all_to_all(spread, ('gx', 'gy'), 0, 0, tiled=True).reshape(512, P_SIZE)  6.03 us
    unnamed x26, local copies, waits for them, and re-layouts  2.68 us
  transfers between devices with their start and end apart: 8, of which 0 were waited for; matrix products, arithmetic and copies ran while one was open for 6% of the time, Pallas kernels for 19%

profile of v5, /device:TPU:1, one launch (start us, length us, event | category | flops | bytes accessed | tf_op | source)
XLA Modules:
  0.0 117.0 jit_solution(18002542887087823699)
XLA Ops:
  0.0 0.7 compare_select_fusion.4
  0.7 0.7 compare_select_fusion.3
  1.4 1.0 copy.20
  2.4 1.2 gather_fusion
  3.6 0.3 fusion
  3.9 0.7 gather_fusion.1
  4.6 3.7 %collective-permute-start.6 = (bf16[288,152]{1,0:T(8,128)(2,1)S(1)}, bf16[288,152]{1,0:T(8,128)(2,1)S(1)}, u32[]{:S(2)}, u32[]{:S(2)}) collective-permute-start(bf16[288,152]{1,0:T(8,128)(2,1)S(1)} %constant_dynamic-update-slice_fusion), channel_id=1, source_target_pairs={{0,16},{1,17},{2,18},{3,19},{4,20},{5,21},{6,22},{7,23},{8,24},{9,... | collective-permute-start | bytes 262664 | tf_op jit(solution)/shard_map/ppermute | solution.py:217
  8.2 0.3 collective-permute-start.5
  8.5 2.9 %collective-permute-start.4 = (bf16[288,152]{1,0:T(8,128)(2,1)S(1)}, bf16[288,152]{1,0:T(8,128)(2,1)S(1)}, u32[]{:S(2)}, u32[]{:S(2)}) collective-permute-start(bf16[288,152]{1,0:T(8,128)(2,1)S(1)} %constant_dynamic-update-slice_fusion), channel_id=1, source_target_pairs={{0,4},{1,5},{2,6},{3,7},{4,0},{5,1},{6,2},{7,3},{8,12},{9,13},{10,... | collective-permute-start | bytes 262664 | tf_op jit(solution)/shard_map/ppermute | solution.py:217
  11.4 3.6 %collective-permute-start.1 = (bf16[288,152]{1,0:T(8,128)(2,1)S(1)}, bf16[288,152]{1,0:T(8,128)(2,1)S(1)}, u32[]{:S(2)}, u32[]{:S(2)}) collective-permute-start(bf16[288,152]{1,0:T(8,128)(2,1)S(1)} %constant_dynamic-update-slice_fusion), channel_id=1, source_target_pairs={{0,64},{32,96},{64,0},{96,32},{1,65},{33,97},{65,1},{97,33},{2,66}... | collective-permute-start | bytes 262664 | tf_op jit(solution)/shard_map/ppermute | solution.py:217
  15.0 0.7 collective-permute-start
  15.8 0.2 fusion.1
  16.0 0.8 broadcast_in_dim.34
  16.9 6.0 %all-to-all-start = ((bf16[128,4,152]{2,1,0:T(4,128)(2,1)}), bf16[128,4,152]{2,1,0:T(4,128)(2,1)S(1)}, u32[]{:S(2)}, u32[]{:S(2)}) async-start(bf16[128,4,152]{2,1,0:T(4,128)(2,1)} %broadcast_in_dim.34), calls=%async_computation | async-start | bytes 524288 | tf_op jit(solution)/shard_map/all_to_all | solution.py:253
  22.9 1.1 compare_select_fusion.1
  24.2 0.9 compare_select_fusion.2
  25.0 0.7 add_select_fusion
  25.7 0.1 copy.24
  25.9 0.7 reshape.49.plane_ref
  26.6 0.1 copy.23
  26.8 0.1 reshape.24
  26.9 1.5 %collective-permute-start.3 = (bf16[288,152]{1,0:T(8,128)(2,1)S(1)}, bf16[288,152]{1,0:T(8,128)(2,1)S(1)}, u32[]{:S(2)}, u32[]{:S(2)}) collective-permute-start(bf16[288,152]{1,0:T(8,128)(2,1)S(1)} %constant_dynamic-update-slice_fusion), channel_id=1, source_target_pairs={{0,2},{1,3},{2,0},{3,1},{4,6},{5,7},{6,4},{7,5},{8,10},{9,11},{10,... | collective-permute-start | bytes 262664 | tf_op jit(solution)/shard_map/ppermute | solution.py:217
  28.4 0.6 collective-permute-start.2
  29.0 0.8 fusion.2.codes_ref
  29.8 21.7 %shard_map.118.w_ref = bf16[40,160,2048]{2,1,0:T(8,128)(2,1)} custom-call(bf16[152,152,316]{2,1,0:T(8,128)(2,1)} %bitcast.22, bf16[288,152]{1,0:T(8,128)(2,1)} %copy-done.5, bf16[288,152]{1,0:T(8,128)(2,1)} %copy-done.4), custom_call_target="tpu_custom_call" | custom-call | bytes 45000000 | tf_op jit(solution)/shard_map/pallas_call | solution.py:204
  51.5 0.9 reshape.28.coarse_ref
  52.5 0.6 copy-done.6
  53.0 0.1 copy-done.7
  53.1 0.1 copy-done.8
  53.1 0.1 copy-done.9
  53.2 0.7 copy-done.10
  53.9 63.1 %shard_map.119 = f32[152,256]{1,0:T(8,128)} custom-call(s32[40,16,128]{2,1,0:T(8,128)} %fusion.2.codes_ref, s32[40,8,256]{2,1,0:T(8,128)} %copy-done.2, s32[40,1,256]{2,1,0:T(1,128)} %reshape.49.plane_ref, bf16[40,160,2048]{2,1,0:T(8,128)(2,1)} %shard_map.118.w_ref, bf16[256,152]{1,0:T(8,128)(2,1)} %bitcast.25, bf16[288,152]{1,0:T(8,128)(2,1)} %copy-done.10, ...), custom_call_target="tpu_custom_call" | custom-call | flops 4322111488 | bytes 28000000 | tf_op jit(solution)/shard_map/pallas_call | solution.py:134
  (34 shorter events, 0.2 us)
Async XLA Ops:
  0.0 3.6 %copy-start = (bf16[8,152,152]{2,1,0:T(8,128)(2,1)S(1)}, bf16[8,152,152]{2,1,0:T(8,128)(2,1)}, u32[]{:S(2)}) copy-start(bf16[8,152,152]{2,1,0:T(8,128)(2,1)} %param.13) | copy-start | bytes 1108996
  2.4 49.1 %copy-start.1 = (bf16[152,256]{0,1:T(8,128)(2,1)}, bf16[152,256]{0,1:T(8,128)(2,1)S(1)}, u32[]{:S(2)}) copy-start(bf16[152,256]{0,1:T(8,128)(2,1)S(1)} %copy.20) | copy-start | bytes 233476
  3.9 48.6 %copy-start.3 = (bf16[152,32]{0,1:T(8,128)(2,1)}, bf16[152,32]{0,1:T(8,128)(2,1)S(1)}, u32[]{:S(2)}) copy-start(bf16[152,32]{0,1:T(8,128)(2,1)S(1)} %fusion) | copy-start | bytes 29188
  4.6 47.8 %collective-permute-start.6 = (bf16[288,152]{1,0:T(8,128)(2,1)S(1)}, bf16[288,152]{1,0:T(8,128)(2,1)S(1)}, u32[]{:S(2)}, u32[]{:S(2)}) collective-permute-start(bf16[288,152]{1,0:T(8,128)(2,1)S(1)} %constant_dynamic-update-slice_fusion), channel_id=1, source_target_pairs={{0,16},{1,17},{2,18},{3,19},{4,20},{5,21},{6,22},{7,23},{8,24},{9,... | collective-permute-start | bytes 262664 | tf_op jit(solution)/shard_map/ppermute | solution.py:217
  8.2 44.2 %collective-permute-start.5 = (bf16[288,152]{1,0:T(8,128)(2,1)S(1)}, bf16[288,152]{1,0:T(8,128)(2,1)S(1)}, u32[]{:S(2)}, u32[]{:S(2)}) collective-permute-start(bf16[288,152]{1,0:T(8,128)(2,1)S(1)} %constant_dynamic-update-slice_fusion), channel_id=1, source_target_pairs={{0,8},{1,9},{2,10},{3,11},{4,12},{5,13},{6,14},{7,15},{8,0},{9,1},... | collective-permute-start | bytes 262664 | tf_op jit(solution)/shard_map/ppermute | solution.py:217
  8.5 43.9 %collective-permute-start.4 = (bf16[288,152]{1,0:T(8,128)(2,1)S(1)}, bf16[288,152]{1,0:T(8,128)(2,1)S(1)}, u32[]{:S(2)}, u32[]{:S(2)}) collective-permute-start(bf16[288,152]{1,0:T(8,128)(2,1)S(1)} %constant_dynamic-update-slice_fusion), channel_id=1, source_target_pairs={{0,4},{1,5},{2,6},{3,7},{4,0},{5,1},{6,2},{7,3},{8,12},{9,13},{10,... | collective-permute-start | bytes 262664 | tf_op jit(solution)/shard_map/ppermute | solution.py:217
  11.4 15.5 %collective-permute-start.1 = (bf16[288,152]{1,0:T(8,128)(2,1)S(1)}, bf16[288,152]{1,0:T(8,128)(2,1)S(1)}, u32[]{:S(2)}, u32[]{:S(2)}) collective-permute-start(bf16[288,152]{1,0:T(8,128)(2,1)S(1)} %constant_dynamic-update-slice_fusion), channel_id=1, source_target_pairs={{0,64},{32,96},{64,0},{96,32},{1,65},{33,97},{65,1},{97,33},{2,66}... | collective-permute-start | bytes 262664 | tf_op jit(solution)/shard_map/ppermute | solution.py:217
  15.0 13.3 %collective-permute-start = (bf16[288,152]{1,0:T(8,128)(2,1)S(1)}, bf16[288,152]{1,0:T(8,128)(2,1)S(1)}, u32[]{:S(2)}, u32[]{:S(2)}) collective-permute-start(bf16[288,152]{1,0:T(8,128)(2,1)S(1)} %constant_dynamic-update-slice_fusion), channel_id=1, source_target_pairs={{0,32},{32,0},{64,96},{96,64},{1,33},{33,1},{65,97},{97,65},{2,34}... | collective-permute-start | bytes 262664 | tf_op jit(solution)/shard_map/ppermute | solution.py:217
  16.9 34.6 %all-to-all-start = ((bf16[128,4,152]{2,1,0:T(4,128)(2,1)}), bf16[128,4,152]{2,1,0:T(4,128)(2,1)S(1)}, u32[]{:S(2)}, u32[]{:S(2)}) async-start(bf16[128,4,152]{2,1,0:T(4,128)(2,1)} %broadcast_in_dim.34), calls=%async_computation | async-start | bytes 524288 | tf_op jit(solution)/shard_map/all_to_all | solution.py:253
  24.1 28.4 %copy-start.2 = (s32[40,8,256]{2,1,0:T(8,128)}, s32[40,8,256]{2,1,0:T(8,128)S(1)}, u32[]{:S(2)}) copy-start(s32[40,8,256]{2,1,0:T(8,128)S(1)} %pad_bitcast_fusion.lanes_ref) | copy-start | bytes 983044
  26.9 2.9 %copy-start.4 = (bf16[288,152]{1,0:T(8,128)(2,1)}, bf16[288,152]{1,0:T(8,128)(2,1)S(1)}, u32[]{:S(2)}) copy-start(bf16[288,152]{1,0:T(8,128)(2,1)S(1)} %collective-permute-done.1.refs_1_.g6) | copy-start | bytes 262660
  26.9 25.5 %collective-permute-start.3 = (bf16[288,152]{1,0:T(8,128)(2,1)S(1)}, bf16[288,152]{1,0:T(8,128)(2,1)S(1)}, u32[]{:S(2)}, u32[]{:S(2)}) collective-permute-start(bf16[288,152]{1,0:T(8,128)(2,1)S(1)} %constant_dynamic-update-slice_fusion), channel_id=1, source_target_pairs={{0,2},{1,3},{2,0},{3,1},{4,6},{5,7},{6,4},{7,5},{8,10},{9,11},{10,... | collective-permute-start | bytes 262664 | tf_op jit(solution)/shard_map/ppermute | solution.py:217
  28.4 1.4 %copy-start.5 = (bf16[288,152]{1,0:T(8,128)(2,1)}, bf16[288,152]{1,0:T(8,128)(2,1)S(1)}, u32[]{:S(2)}) copy-start(bf16[288,152]{1,0:T(8,128)(2,1)S(1)} %collective-permute-done.refs_0_.g5) | copy-start | bytes 262660
  28.4 24.1 %collective-permute-start.2 = (bf16[288,152]{1,0:T(8,128)(2,1)S(1)}, bf16[288,152]{1,0:T(8,128)(2,1)S(1)}, u32[]{:S(2)}, u32[]{:S(2)}) collective-permute-start(bf16[288,152]{1,0:T(8,128)(2,1)S(1)} %constant_dynamic-update-slice_fusion), channel_id=1, source_target_pairs={{0,1},{1,0},{2,3},{3,2},{4,5},{5,4},{6,7},{7,6},{8,9},{9,8},{10,11... | collective-permute-start | bytes 262664 | tf_op jit(solution)/shard_map/ppermute | solution.py:217
  52.4 0.6 copy-start.6
  52.4 0.7 copy-start.7
  52.4 0.7 copy-start.8
  52.4 0.8 copy-start.9
  53.2 0.7 copy-start.10

commit v6 on v5

--- a/solution.py
+++ b/solution.py
@@ -243,8 +243,8 @@
     coarse_mult = upward(up_matrices, parent_mult).T
     outgoing = jnp.concatenate(
         [
-            own.at[send_leaf].get(mode="promise_in_bounds"),
-            parent_own.at[send_parent].get(mode="promise_in_bounds"),
+            own.at[send_leaf].get(mode="promise_in_bounds", wrap_negative_indices=False),
+            parent_own.at[send_parent].get(mode="promise_in_bounds", wrap_negative_indices=False),
         ],
         axis=0,
     )

time: 117 us -> 117 us (level)
    select_n x2 -> x0, other arithmetic: 1.4 us -> none  [the longest x1 0.72 us: shards(): parent_own.at[send_parent].get(mode='promise_in_bounds')]
where the time goes in v6:
time: 117 us; the launch traced here: 116 us
  Pallas kernels  84.8 us (72%)
  starting transfers between devices  19.4 us (17%)
  local copies, waits for them, and re-layouts  7.24 us (6%)
  other arithmetic  4.26 us (4%)
    pallas_call x1, Pallas kernels, main_call(): pl.pallas_call(main_kernel, in_specs=[anyspec, vm, vm, anyspec] + [vm] *...  63.1 us
    pallas_call x1, Pallas kernels, relay(): pl.pallas_call(relay_kernel, grid=(steps,), in_specs=[pl.BlockSpec((PBLOC...  21.7 us
    ppermute x7, starting transfers between devices, swapped(): lax.ppermute(array, axis, [(i, i ^ 1 << distance) for i in range(lax.axis...  13.3 us
    all_to_all x1, starting transfers between devices, shards(): lax.all_to_all(spread, ('gx', 'gy'), 0, 0, tiled=True).reshape(512, P_SIZE)  6.04 us
    unnamed x26, local copies, waits for them, and re-layouts  2.74 us
  transfers between devices with their start and end apart: 8, of which 0 were waited for; matrix products, arithmetic and copies ran while one was open for 6% of the time, Pallas kernels for 19%

profile of v6, /device:TPU:1, one launch (start us, length us, event | category | flops | bytes accessed | tf_op | source)
XLA Modules:
  0.0 116.4 jit_solution(12107027756076360733)
XLA Ops:
  0.0 1.0 copy.20
  1.1 0.8 pad_clamp_fusion
  1.8 1.1 gather_fusion
  3.0 0.3 fusion
  3.3 0.7 gather_fusion.1
  3.9 3.7 %collective-permute-start.6 = (bf16[288,152]{1,0:T(8,128)(2,1)S(1)}, bf16[288,152]{1,0:T(8,128)(2,1)S(1)}, u32[]{:S(2)}, u32[]{:S(2)}) collective-permute-start(bf16[288,152]{1,0:T(8,128)(2,1)S(1)} %constant_dynamic-update-slice_fusion), channel_id=1, source_target_pairs={{0,16},{1,17},{2,18},{3,19},{4,20},{5,21},{6,22},{7,23},{8,24},{9,... | collective-permute-start | bytes 262664 | tf_op jit(solution)/shard_map/ppermute | solution.py:217
  7.6 0.3 collective-permute-start.5
  7.9 2.9 %collective-permute-start.4 = (bf16[288,152]{1,0:T(8,128)(2,1)S(1)}, bf16[288,152]{1,0:T(8,128)(2,1)S(1)}, u32[]{:S(2)}, u32[]{:S(2)}) collective-permute-start(bf16[288,152]{1,0:T(8,128)(2,1)S(1)} %constant_dynamic-update-slice_fusion), channel_id=1, source_target_pairs={{0,4},{1,5},{2,6},{3,7},{4,0},{5,1},{6,2},{7,3},{8,12},{9,13},{10,... | collective-permute-start | bytes 262664 | tf_op jit(solution)/shard_map/ppermute | solution.py:217
  10.8 3.6 %collective-permute-start.1 = (bf16[288,152]{1,0:T(8,128)(2,1)S(1)}, bf16[288,152]{1,0:T(8,128)(2,1)S(1)}, u32[]{:S(2)}, u32[]{:S(2)}) collective-permute-start(bf16[288,152]{1,0:T(8,128)(2,1)S(1)} %constant_dynamic-update-slice_fusion), channel_id=1, source_target_pairs={{0,64},{32,96},{64,0},{96,32},{1,65},{33,97},{65,1},{97,33},{2,66}... | collective-permute-start | bytes 262664 | tf_op jit(solution)/shard_map/ppermute | solution.py:217
  14.4 0.7 collective-permute-start
  15.2 0.2 fusion.1
  15.4 0.8 broadcast_in_dim.34
  16.3 6.0 %all-to-all-start = ((bf16[128,4,152]{2,1,0:T(4,128)(2,1)}), bf16[128,4,152]{2,1,0:T(4,128)(2,1)S(1)}, u32[]{:S(2)}, u32[]{:S(2)}) async-start(bf16[128,4,152]{2,1,0:T(4,128)(2,1)} %broadcast_in_dim.34), calls=%async_computation | async-start | bytes 524288 | tf_op jit(solution)/shard_map/all_to_all | solution.py:253
  22.3 1.1 compare_select_fusion.1
  23.6 0.9 compare_select_fusion.2
  24.4 0.7 add_select_fusion
  25.1 0.1 copy.24
  25.3 0.7 reshape.49.plane_ref
  26.0 0.1 copy.23
  26.2 0.1 reshape.24
  26.3 0.0 collective-permute-done.1.refs_1_.g6
  26.3 1.5 %collective-permute-start.3 = (bf16[288,152]{1,0:T(8,128)(2,1)S(1)}, bf16[288,152]{1,0:T(8,128)(2,1)S(1)}, u32[]{:S(2)}, u32[]{:S(2)}) collective-permute-start(bf16[288,152]{1,0:T(8,128)(2,1)S(1)} %constant_dynamic-update-slice_fusion), channel_id=1, source_target_pairs={{0,2},{1,3},{2,0},{3,1},{4,6},{5,7},{6,4},{7,5},{8,10},{9,11},{10,... | collective-permute-start | bytes 262664 | tf_op jit(solution)/shard_map/ppermute | solution.py:217
  27.8 0.6 collective-permute-start.2
  28.4 0.8 fusion.2.codes_ref
  29.2 21.7 %shard_map.118.w_ref = bf16[40,160,2048]{2,1,0:T(8,128)(2,1)} custom-call(bf16[152,152,316]{2,1,0:T(8,128)(2,1)} %bitcast.22, bf16[288,152]{1,0:T(8,128)(2,1)} %copy-done.5, bf16[288,152]{1,0:T(8,128)(2,1)} %copy-done.4), custom_call_target="tpu_custom_call" | custom-call | bytes 45000000 | tf_op jit(solution)/shard_map/pallas_call | solution.py:204
  50.9 0.9 reshape.28.coarse_ref
  51.9 0.6 copy-done.6
  52.4 0.1 copy-done.7
  52.5 0.1 copy-done.8
  52.5 0.1 copy-done.9
  52.6 0.7 copy-done.10
  53.3 63.1 %shard_map.119 = f32[152,256]{1,0:T(8,128)} custom-call(s32[40,16,128]{2,1,0:T(8,128)} %fusion.2.codes_ref, s32[40,8,256]{2,1,0:T(8,128)} %copy-done.2, s32[40,1,256]{2,1,0:T(1,128)} %reshape.49.plane_ref, bf16[40,160,2048]{2,1,0:T(8,128)(2,1)} %shard_map.118.w_ref, bf16[256,152]{1,0:T(8,128)(2,1)} %bitcast.25, bf16[288,152]{1,0:T(8,128)(2,1)} %copy-done.10, ...), custom_call_target="tpu_custom_call" | custom-call | flops 4322111488 | bytes 28000000 | tf_op jit(solution)/shard_map/pallas_call | solution.py:134
  (32 shorter events, 0.2 us)
Async XLA Ops:
  0.0 3.0 %copy-start = (bf16[8,152,152]{2,1,0:T(8,128)(2,1)S(1)}, bf16[8,152,152]{2,1,0:T(8,128)(2,1)}, u32[]{:S(2)}) copy-start(bf16[8,152,152]{2,1,0:T(8,128)(2,1)} %param.13) | copy-start | bytes 1108996
  1.1 49.8 %copy-start.1 = (bf16[152,256]{0,1:T(8,128)(2,1)}, bf16[152,256]{0,1:T(8,128)(2,1)S(1)}, u32[]{:S(2)}) copy-start(bf16[152,256]{0,1:T(8,128)(2,1)S(1)} %copy.20) | copy-start | bytes 233476
  3.3 48.6 %copy-start.3 = (bf16[152,32]{0,1:T(8,128)(2,1)}, bf16[152,32]{0,1:T(8,128)(2,1)S(1)}, u32[]{:S(2)}) copy-start(bf16[152,32]{0,1:T(8,128)(2,1)S(1)} %fusion) | copy-start | bytes 29188
  3.9 47.8 %collective-permute-start.6 = (bf16[288,152]{1,0:T(8,128)(2,1)S(1)}, bf16[288,152]{1,0:T(8,128)(2,1)S(1)}, u32[]{:S(2)}, u32[]{:S(2)}) collective-permute-start(bf16[288,152]{1,0:T(8,128)(2,1)S(1)} %constant_dynamic-update-slice_fusion), channel_id=1, source_target_pairs={{0,16},{1,17},{2,18},{3,19},{4,20},{5,21},{6,22},{7,23},{8,24},{9,... | collective-permute-start | bytes 262664 | tf_op jit(solution)/shard_map/ppermute | solution.py:217
  7.6 44.2 %collective-permute-start.5 = (bf16[288,152]{1,0:T(8,128)(2,1)S(1)}, bf16[288,152]{1,0:T(8,128)(2,1)S(1)}, u32[]{:S(2)}, u32[]{:S(2)}) collective-permute-start(bf16[288,152]{1,0:T(8,128)(2,1)S(1)} %constant_dynamic-update-slice_fusion), channel_id=1, source_target_pairs={{0,8},{1,9},{2,10},{3,11},{4,12},{5,13},{6,14},{7,15},{8,0},{9,1},... | collective-permute-start | bytes 262664 | tf_op jit(solution)/shard_map/ppermute | solution.py:217
  7.9 43.9 %collective-permute-start.4 = (bf16[288,152]{1,0:T(8,128)(2,1)S(1)}, bf16[288,152]{1,0:T(8,128)(2,1)S(1)}, u32[]{:S(2)}, u32[]{:S(2)}) collective-permute-start(bf16[288,152]{1,0:T(8,128)(2,1)S(1)} %constant_dynamic-update-slice_fusion), channel_id=1, source_target_pairs={{0,4},{1,5},{2,6},{3,7},{4,0},{5,1},{6,2},{7,3},{8,12},{9,13},{10,... | collective-permute-start | bytes 262664 | tf_op jit(solution)/shard_map/ppermute | solution.py:217
  10.8 15.5 %collective-permute-start.1 = (bf16[288,152]{1,0:T(8,128)(2,1)S(1)}, bf16[288,152]{1,0:T(8,128)(2,1)S(1)}, u32[]{:S(2)}, u32[]{:S(2)}) collective-permute-start(bf16[288,152]{1,0:T(8,128)(2,1)S(1)} %constant_dynamic-update-slice_fusion), channel_id=1, source_target_pairs={{0,64},{32,96},{64,0},{96,32},{1,65},{33,97},{65,1},{97,33},{2,66}... | collective-permute-start | bytes 262664 | tf_op jit(solution)/shard_map/ppermute | solution.py:217
  14.4 13.3 %collective-permute-start = (bf16[288,152]{1,0:T(8,128)(2,1)S(1)}, bf16[288,152]{1,0:T(8,128)(2,1)S(1)}, u32[]{:S(2)}, u32[]{:S(2)}) collective-permute-start(bf16[288,152]{1,0:T(8,128)(2,1)S(1)} %constant_dynamic-update-slice_fusion), channel_id=1, source_target_pairs={{0,32},{32,0},{64,96},{96,64},{1,33},{33,1},{65,97},{97,65},{2,34}... | collective-permute-start | bytes 262664 | tf_op jit(solution)/shard_map/ppermute | solution.py:217
  16.3 34.6 %all-to-all-start = ((bf16[128,4,152]{2,1,0:T(4,128)(2,1)}), bf16[128,4,152]{2,1,0:T(4,128)(2,1)S(1)}, u32[]{:S(2)}, u32[]{:S(2)}) async-start(bf16[128,4,152]{2,1,0:T(4,128)(2,1)} %broadcast_in_dim.34), calls=%async_computation | async-start | bytes 524288 | tf_op jit(solution)/shard_map/all_to_all | solution.py:253
  23.5 28.4 %copy-start.2 = (s32[40,8,256]{2,1,0:T(8,128)}, s32[40,8,256]{2,1,0:T(8,128)S(1)}, u32[]{:S(2)}) copy-start(s32[40,8,256]{2,1,0:T(8,128)S(1)} %pad_bitcast_fusion.lanes_ref) | copy-start | bytes 983044
  26.3 2.9 %copy-start.4 = (bf16[288,152]{1,0:T(8,128)(2,1)}, bf16[288,152]{1,0:T(8,128)(2,1)S(1)}, u32[]{:S(2)}) copy-start(bf16[288,152]{1,0:T(8,128)(2,1)S(1)} %collective-permute-done.1.refs_1_.g6) | copy-start | bytes 262660
  26.3 25.5 %collective-permute-start.3 = (bf16[288,152]{1,0:T(8,128)(2,1)S(1)}, bf16[288,152]{1,0:T(8,128)(2,1)S(1)}, u32[]{:S(2)}, u32[]{:S(2)}) collective-permute-start(bf16[288,152]{1,0:T(8,128)(2,1)S(1)} %constant_dynamic-update-slice_fusion), channel_id=1, source_target_pairs={{0,2},{1,3},{2,0},{3,1},{4,6},{5,7},{6,4},{7,5},{8,10},{9,11},{10,... | collective-permute-start | bytes 262664 | tf_op jit(solution)/shard_map/ppermute | solution.py:217
  27.8 1.4 %copy-start.5 = (bf16[288,152]{1,0:T(8,128)(2,1)}, bf16[288,152]{1,0:T(8,128)(2,1)S(1)}, u32[]{:S(2)}) copy-start(bf16[288,152]{1,0:T(8,128)(2,1)S(1)} %collective-permute-done.refs_0_.g5) | copy-start | bytes 262660
  27.8 24.1 %collective-permute-start.2 = (bf16[288,152]{1,0:T(8,128)(2,1)S(1)}, bf16[288,152]{1,0:T(8,128)(2,1)S(1)}, u32[]{:S(2)}, u32[]{:S(2)}) collective-permute-start(bf16[288,152]{1,0:T(8,128)(2,1)S(1)} %constant_dynamic-update-slice_fusion), channel_id=1, source_target_pairs={{0,1},{1,0},{2,3},{3,2},{4,5},{5,4},{6,7},{7,6},{8,9},{9,8},{10,11... | collective-permute-start | bytes 262664 | tf_op jit(solution)/shard_map/ppermute | solution.py:217
  51.8 0.6 copy-start.6
  51.8 0.7 copy-start.7
  51.8 0.7 copy-start.8
  51.8 0.8 copy-start.9
  52.6 0.7 copy-start.10

commit v7 on v6

--- a/solution.py
+++ b/solution.py
@@ -49,7 +49,7 @@
         wide = widened(g[0:LEAVES, :])
         fill(LEAVES * b, wide)
         columns[:, LEAVES * b:LEAVES * (b + 1)] = wide.T[0:PADDED].astype(jnp.bfloat16)
-    fill(2048, widened(coarse_ref[...]))
+    fill(2048, widened(coarse_ref[...].astype(jnp.float32).reshape(512, P_SIZE)))
     flat[2 * ZERO:2 * TABLE, :] = jnp.zeros((2 * (TABLE - ZERO), 128), jnp.float32)
     parents = jnp.concatenate([pown_ref[...].astype(jnp.float32)] + [g[LEAVES:LEAVES + PARENTS, :].astype(jnp.float32) for g in (g0, g1, g2, g3, g4, g5, g6)], axis=0)
     ptable[...] = widened(parents).T.astype(jnp.bfloat16)
@@ -250,7 +250,7 @@
     )
     ghosts = [swapped(outgoing, "gy", b) for b in range(5)] + [swapped(outgoing, "gx", b) for b in range(2)]
     spread = jnp.broadcast_to(coarse_mult[None], (128, 4, P_SIZE))
-    coarse_all = lax.all_to_all(spread, ("gx", "gy"), 0, 0, tiled=True).reshape(512, P_SIZE)
+    coarse_all = lax.all_to_all(spread, ("gx", "gy"), 0, 0, tiled=True)
     matrices = relay(far_matrices, 0, PADDED, ghosts[5:7])
     codes, lanes, plane = tables(codes_leaf, valid_leaf, codes_parent, valid_parent, codes_coarse, valid_coarse)
     return main_call(codes, lanes, plane, matrices, own, ghosts, parent_own, coarse_all, down_matrices)

time: 117 us -> 116 us (level)
    unnamed x26 -> x28, local copies, waits for them, and re-layouts: 2.74 us -> 2.8 us
  transfers between devices with their start and end apart: 8 -> 8, of which waited for: 0 -> 0; matrix products, arithmetic and copies ran while one was open for 6% -> 5% of each run, Pallas kernels for 19% -> 19%
where the time goes in v7:
time: 116 us; the launch traced here: 115 us
  Pallas kernels  84.7 us (73%)
  starting transfers between devices  19.4 us (17%)
  local copies, waits for them, and re-layouts  6.41 us (6%)
  other arithmetic  4.25 us (4%)
    pallas_call x1, Pallas kernels, main_call(): pl.pallas_call(main_kernel, in_specs=[anyspec, vm, vm, anyspec] + [vm] *...  63.1 us
    pallas_call x1, Pallas kernels, relay(): pl.pallas_call(relay_kernel, grid=(steps,), in_specs=[pl.BlockSpec((PBLOC...  21.6 us
    ppermute x7, starting transfers between devices, swapped(): lax.ppermute(array, axis, [(i, i ^ 1 << distance) for i in range(lax.axis...  13.3 us
    all_to_all x1, starting transfers between devices, shards(): coarse_all = lax.all_to_all(spread, ('gx', 'gy'), 0, 0, tiled=True)  6.04 us
    unnamed x28, local copies, waits for them, and re-layouts  2.8 us
  transfers between devices with their start and end apart: 8, of which 0 were waited for; matrix products, arithmetic and copies ran while one was open for 5% of the time, Pallas kernels for 19%

profile of v7, /device:TPU:1, one launch (start us, length us, event | category | flops | bytes accessed | tf_op | source)
XLA Modules:
  0.0 115.5 jit_solution(226172720972745931)
XLA Ops:
  0.0 1.0 copy.20
  1.1 0.8 pad_clamp_fusion
  1.8 1.1 gather_fusion
  3.0 0.3 fusion
  3.3 0.7 gather_fusion.1
  3.9 3.7 %collective-permute-start.6 = (bf16[288,152]{1,0:T(8,128)(2,1)S(1)}, bf16[288,152]{1,0:T(8,128)(2,1)S(1)}, u32[]{:S(2)}, u32[]{:S(2)}) collective-permute-start(bf16[288,152]{1,0:T(8,128)(2,1)S(1)} %constant_dynamic-update-slice_fusion), channel_id=1, source_target_pairs={{0,16},{1,17},{2,18},{3,19},{4,20},{5,21},{6,22},{7,23},{8,24},{9,... | collective-permute-start | bytes 262664 | tf_op jit(solution)/shard_map/ppermute | solution.py:217
  7.6 0.3 collective-permute-start.5
  7.9 2.9 %collective-permute-start.4 = (bf16[288,152]{1,0:T(8,128)(2,1)S(1)}, bf16[288,152]{1,0:T(8,128)(2,1)S(1)}, u32[]{:S(2)}, u32[]{:S(2)}) collective-permute-start(bf16[288,152]{1,0:T(8,128)(2,1)S(1)} %constant_dynamic-update-slice_fusion), channel_id=1, source_target_pairs={{0,4},{1,5},{2,6},{3,7},{4,0},{5,1},{6,2},{7,3},{8,12},{9,13},{10,... | collective-permute-start | bytes 262664 | tf_op jit(solution)/shard_map/ppermute | solution.py:217
  10.8 3.6 %collective-permute-start.1 = (bf16[288,152]{1,0:T(8,128)(2,1)S(1)}, bf16[288,152]{1,0:T(8,128)(2,1)S(1)}, u32[]{:S(2)}, u32[]{:S(2)}) collective-permute-start(bf16[288,152]{1,0:T(8,128)(2,1)S(1)} %constant_dynamic-update-slice_fusion), channel_id=1, source_target_pairs={{0,64},{32,96},{64,0},{96,32},{1,65},{33,97},{65,1},{97,33},{2,66}... | collective-permute-start | bytes 262664 | tf_op jit(solution)/shard_map/ppermute | solution.py:217
  14.4 0.7 collective-permute-start
  15.2 0.2 fusion.1
  15.4 0.8 broadcast_in_dim.34
  16.3 6.0 %all-to-all-start = ((bf16[128,4,152]{2,1,0:T(4,128)(2,1)}), bf16[128,4,152]{2,1,0:T(4,128)(2,1)S(1)}, u32[]{:S(2)}, u32[]{:S(2)}) async-start(bf16[128,4,152]{2,1,0:T(4,128)(2,1)} %broadcast_in_dim.34), calls=%async_computation | async-start | bytes 524288 | tf_op jit(solution)/shard_map/all_to_all | solution.py:253
  22.3 1.1 compare_select_fusion.1
  23.5 0.9 compare_select_fusion.2
  24.4 0.7 add_select_fusion
  25.1 0.1 copy.24
  25.3 0.7 reshape.45.plane_ref
  26.0 0.1 copy.23
  26.2 0.1 reshape.21
  26.3 0.0 collective-permute-done.1.refs_1_.g6
  26.3 1.5 %collective-permute-start.3 = (bf16[288,152]{1,0:T(8,128)(2,1)S(1)}, bf16[288,152]{1,0:T(8,128)(2,1)S(1)}, u32[]{:S(2)}, u32[]{:S(2)}) collective-permute-start(bf16[288,152]{1,0:T(8,128)(2,1)S(1)} %constant_dynamic-update-slice_fusion), channel_id=1, source_target_pairs={{0,2},{1,3},{2,0},{3,1},{4,6},{5,7},{6,4},{7,5},{8,10},{9,11},{10,... | collective-permute-start | bytes 262664 | tf_op jit(solution)/shard_map/ppermute | solution.py:217
  27.8 0.6 collective-permute-start.2
  28.4 0.8 fusion.2.codes_ref
  29.2 21.6 %shard_map.118.w_ref = bf16[40,160,2048]{2,1,0:T(8,128)(2,1)} custom-call(bf16[152,152,316]{2,1,0:T(8,128)(2,1)} %bitcast.22, bf16[288,152]{1,0:T(8,128)(2,1)} %copy-done.6, bf16[288,152]{1,0:T(8,128)(2,1)} %copy-done.5), custom_call_target="tpu_custom_call" | custom-call | bytes 45000000 | tf_op jit(solution)/shard_map/pallas_call | solution.py:204
  50.9 0.5 copy-done.7
  51.4 0.1 copy-done.8
  51.5 0.1 copy-done.9
  51.5 0.1 copy-done.10
  51.6 0.0 copy-done.11
  51.6 0.7 copy-done.4
  52.4 63.1 %shard_map.119 = f32[152,256]{1,0:T(8,128)} custom-call(s32[40,16,128]{2,1,0:T(8,128)} %fusion.2.codes_ref, s32[40,8,256]{2,1,0:T(8,128)} %copy-done.2, s32[40,1,256]{2,1,0:T(1,128)} %reshape.45.plane_ref, bf16[40,160,2048]{2,1,0:T(8,128)(2,1)} %shard_map.118.w_ref, bf16[256,152]{1,0:T(8,128)(2,1)} %bitcast.25, bf16[288,152]{1,0:T(8,128)(2,1)} %copy-done.11, ...), custom_call_target="tpu_custom_call" | custom-call | flops 4322111488 | bytes 28000000 | tf_op jit(solution)/shard_map/pallas_call | solution.py:134
  (33 shorter events, 0.2 us)
Async XLA Ops:
  0.0 3.0 %copy-start = (bf16[8,152,152]{2,1,0:T(8,128)(2,1)S(1)}, bf16[8,152,152]{2,1,0:T(8,128)(2,1)}, u32[]{:S(2)}) copy-start(bf16[8,152,152]{2,1,0:T(8,128)(2,1)} %param.13) | copy-start | bytes 1108996
  1.1 49.7 %copy-start.1 = (bf16[152,256]{0,1:T(8,128)(2,1)}, bf16[152,256]{0,1:T(8,128)(2,1)S(1)}, u32[]{:S(2)}) copy-start(bf16[152,256]{0,1:T(8,128)(2,1)S(1)} %copy.20) | copy-start | bytes 233476
  3.3 47.6 %copy-start.3 = (bf16[152,32]{0,1:T(8,128)(2,1)}, bf16[152,32]{0,1:T(8,128)(2,1)S(1)}, u32[]{:S(2)}) copy-start(bf16[152,32]{0,1:T(8,128)(2,1)S(1)} %fusion) | copy-start | bytes 29188
  3.9 46.8 %collective-permute-start.6 = (bf16[288,152]{1,0:T(8,128)(2,1)S(1)}, bf16[288,152]{1,0:T(8,128)(2,1)S(1)}, u32[]{:S(2)}, u32[]{:S(2)}) collective-permute-start(bf16[288,152]{1,0:T(8,128)(2,1)S(1)} %constant_dynamic-update-slice_fusion), channel_id=1, source_target_pairs={{0,16},{1,17},{2,18},{3,19},{4,20},{5,21},{6,22},{7,23},{8,24},{9,... | collective-permute-start | bytes 262664 | tf_op jit(solution)/shard_map/ppermute | solution.py:217
  7.6 43.2 %collective-permute-start.5 = (bf16[288,152]{1,0:T(8,128)(2,1)S(1)}, bf16[288,152]{1,0:T(8,128)(2,1)S(1)}, u32[]{:S(2)}, u32[]{:S(2)}) collective-permute-start(bf16[288,152]{1,0:T(8,128)(2,1)S(1)} %constant_dynamic-update-slice_fusion), channel_id=1, source_target_pairs={{0,8},{1,9},{2,10},{3,11},{4,12},{5,13},{6,14},{7,15},{8,0},{9,1},... | collective-permute-start | bytes 262664 | tf_op jit(solution)/shard_map/ppermute | solution.py:217
  7.9 42.9 %collective-permute-start.4 = (bf16[288,152]{1,0:T(8,128)(2,1)S(1)}, bf16[288,152]{1,0:T(8,128)(2,1)S(1)}, u32[]{:S(2)}, u32[]{:S(2)}) collective-permute-start(bf16[288,152]{1,0:T(8,128)(2,1)S(1)} %constant_dynamic-update-slice_fusion), channel_id=1, source_target_pairs={{0,4},{1,5},{2,6},{3,7},{4,0},{5,1},{6,2},{7,3},{8,12},{9,13},{10,... | collective-permute-start | bytes 262664 | tf_op jit(solution)/shard_map/ppermute | solution.py:217
  10.8 15.5 %collective-permute-start.1 = (bf16[288,152]{1,0:T(8,128)(2,1)S(1)}, bf16[288,152]{1,0:T(8,128)(2,1)S(1)}, u32[]{:S(2)}, u32[]{:S(2)}) collective-permute-start(bf16[288,152]{1,0:T(8,128)(2,1)S(1)} %constant_dynamic-update-slice_fusion), channel_id=1, source_target_pairs={{0,64},{32,96},{64,0},{96,32},{1,65},{33,97},{65,1},{97,33},{2,66}... | collective-permute-start | bytes 262664 | tf_op jit(solution)/shard_map/ppermute | solution.py:217
  14.4 13.3 %collective-permute-start = (bf16[288,152]{1,0:T(8,128)(2,1)S(1)}, bf16[288,152]{1,0:T(8,128)(2,1)S(1)}, u32[]{:S(2)}, u32[]{:S(2)}) collective-permute-start(bf16[288,152]{1,0:T(8,128)(2,1)S(1)} %constant_dynamic-update-slice_fusion), channel_id=1, source_target_pairs={{0,32},{32,0},{64,96},{96,64},{1,33},{33,1},{65,97},{97,65},{2,34}... | collective-permute-start | bytes 262664 | tf_op jit(solution)/shard_map/ppermute | solution.py:217
  16.3 34.6 %all-to-all-start = ((bf16[128,4,152]{2,1,0:T(4,128)(2,1)}), bf16[128,4,152]{2,1,0:T(4,128)(2,1)S(1)}, u32[]{:S(2)}, u32[]{:S(2)}) async-start(bf16[128,4,152]{2,1,0:T(4,128)(2,1)} %broadcast_in_dim.34), calls=%async_computation | async-start | bytes 524288 | tf_op jit(solution)/shard_map/all_to_all | solution.py:253
  23.4 27.4 %copy-start.2 = (s32[40,8,256]{2,1,0:T(8,128)}, s32[40,8,256]{2,1,0:T(8,128)S(1)}, u32[]{:S(2)}) copy-start(s32[40,8,256]{2,1,0:T(8,128)S(1)} %pad_bitcast_fusion.lanes_ref) | copy-start | bytes 983044
  26.3 2.9 %copy-start.5 = (bf16[288,152]{1,0:T(8,128)(2,1)}, bf16[288,152]{1,0:T(8,128)(2,1)S(1)}, u32[]{:S(2)}) copy-start(bf16[288,152]{1,0:T(8,128)(2,1)S(1)} %collective-permute-done.1.refs_1_.g6) | copy-start | bytes 262660
  26.3 24.5 %collective-permute-start.3 = (bf16[288,152]{1,0:T(8,128)(2,1)S(1)}, bf16[288,152]{1,0:T(8,128)(2,1)S(1)}, u32[]{:S(2)}, u32[]{:S(2)}) collective-permute-start(bf16[288,152]{1,0:T(8,128)(2,1)S(1)} %constant_dynamic-update-slice_fusion), channel_id=1, source_target_pairs={{0,2},{1,3},{2,0},{3,1},{4,6},{5,7},{6,4},{7,5},{8,10},{9,11},{10,... | collective-permute-start | bytes 262664 | tf_op jit(solution)/shard_map/ppermute | solution.py:217
  27.8 1.4 %copy-start.6 = (bf16[288,152]{1,0:T(8,128)(2,1)}, bf16[288,152]{1,0:T(8,128)(2,1)S(1)}, u32[]{:S(2)}) copy-start(bf16[288,152]{1,0:T(8,128)(2,1)S(1)} %collective-permute-done.refs_0_.g5) | copy-start | bytes 262660
  27.8 23.1 %collective-permute-start.2 = (bf16[288,152]{1,0:T(8,128)(2,1)S(1)}, bf16[288,152]{1,0:T(8,128)(2,1)S(1)}, u32[]{:S(2)}, u32[]{:S(2)}) collective-permute-start(bf16[288,152]{1,0:T(8,128)(2,1)S(1)} %constant_dynamic-update-slice_fusion), channel_id=1, source_target_pairs={{0,1},{1,0},{2,3},{3,2},{4,5},{5,4},{6,7},{7,6},{8,9},{9,8},{10,11... | collective-permute-start | bytes 262664 | tf_op jit(solution)/shard_map/ppermute | solution.py:217
  50.8 0.7 copy-start.7
  50.8 0.7 copy-start.8
  50.8 0.7 copy-start.9
  50.8 0.8 copy-start.10
  50.9 0.8 copy-start.11
  51.6 0.7 copy-start.4
